TPU v7x, 512 devices: a whole 4x4x16 slice. The times are simulated.
512 devices in a mesh: wall: 16 (over z_lo, core), tang: 32 (over z_hi, y, x).
Axes of the slice: x: 4, y: 4, z: 16 (z_hi: 2, z_lo: 8; z = z_hi * 8 + z_lo), core: 2. Of those that a mesh axis runs over, the one named last changes fastest.
Arguments:
- right_side: float32 [32, 64, 384], P('wall', 'tang'), may hold values from -6 to 6
- inverse_blocks: bfloat16 [32, 64, 384, 384], P('wall', 'tang'), as said below
- lower_blocks: bfloat16 [32, 64, 384, 384], P('wall', 'tang'), may hold values from -0.375 to 0.375
- upper_blocks: bfloat16 [32, 64, 384, 384], P('wall', 'tang'), may hold values from -0.375 to 0.375
- trace_map: bfloat16 [384, 384], replicated, may hold values from -0.3125 to 0.3125
- lift_map: bfloat16 [384, 384], replicated, may hold values from -0.3125 to 0.3125
- neighbours: int32 [64, 4], P('tang'), may hold values from 0 to 63, as said below
Outputs:
- correction: float32 [32, 64, 384], P('wall', 'tang')
- face_residual: float32 [32, 64, 384], P('wall', 'tang')
Inputs may be any that keep to these rules, and one draw needn't show every extreme that they name: `inverse_blocks`: given inverses of the factorization's diagonal blocks; entries of order one or less, every block of full rank. Face pairs are symmetric: neighbours[neighbours[l, 0], 1] = l and neighbours[neighbours[l, 2], 3] = l. Lines being split in order over tang, the line across face 0 or 2 lies at the same index of tang or the next one (cyclically), and the line across face 1 or 3 lies at the same index or the previous one.
All inputs are finite; a program needn't handle non-finite values.
Results may differ from a plain program's by a relative error of at most 0.0003.
Values sent between devices are 32-bit elements; how exact they have to be, the bound alone decides.
No kernel may reach another device: no remote copies, remote signals or barrier semaphores. Data moves between devices by JAX's collectives and lax.ppermute only.
A program may use at most 128 MiB of HBM per device.

v0:
```python
import jax
import jax.numpy as jnp
from jax import lax
from jax.sharding import PartitionSpec as P


def entering_2(part, axis, combine, identity, reverse):
    count = lax.axis_size(axis)
    place = lax.axis_index(axis)
    ahead = count - 1 - place if reverse else place
    gathered = jax.tree.map(lambda a: lax.all_gather(a, axis), part)
    state = jax.tree.map(lambda a, e: jnp.zeros_like(a) + jnp.asarray(e, a.dtype), part, identity)

    def one(step, state):
        source = count - 1 - step if reverse else step
        return combine(
            state, jax.tree.map(lambda a: lax.dynamic_index_in_dim(a, source, 0, False), gathered)
        )

    return lax.fori_loop(0, ahead, one, state)


def with_halo(array, sides, width):
    for axis, dim in sides:
        count, length = (lax.axis_size(axis), array.shape[dim])
        up = [(i, (i + 1) % count) for i in range(count)]
        down = [(j, i) for i, j in up]
        last = lax.slice_in_dim(array, length - width, length, axis=dim)
        first = lax.slice_in_dim(array, 0, width, axis=dim)
        before = lax.ppermute(last, axis, up)
        after = lax.ppermute(first, axis, down)
        array = jnp.concatenate([before, array, after], axis=dim)
    return array


def apply_block(matrix, vector):
    return jnp.einsum(
        "lij,lj->li", matrix.astype(jnp.float32), vector, precision=lax.Precision.HIGHEST
    )


def block_times(left, right):
    return jnp.einsum("lij,ljm->lim", left, right, precision=lax.Precision.HIGHEST)


def compose_maps(earlier, later):
    return (later[0] + apply_block(later[1], earlier[0]), block_times(later[1], earlier[1]))


def sweep_down(right_side, inverse_blocks, lower_blocks, entering):
    values = []
    previous = entering
    for cell in range(right_side.shape[0]):
        previous = apply_block(
            inverse_blocks[cell], right_side[cell] - apply_block(lower_blocks[cell], previous)
        )
        values.append(previous)
    return jnp.stack(values, axis=0)


def sweep_up(forward, inverse_blocks, upper_blocks, entering):
    cells_here = forward.shape[0]
    values = [None] * cells_here
    following = entering
    for cell in range(cells_here - 1, -1, -1):
        following = forward[cell] - apply_block(
            inverse_blocks[cell], apply_block(upper_blocks[cell], following)
        )
        values[cell] = following
    return jnp.stack(values, axis=0)


def body(right_side, inverse_blocks, lower_blocks, upper_blocks, trace_map, lift_map, neighbours):
    cells_here, lines_here, width = right_side.shape
    zero_vector = jnp.zeros((lines_here, width), jnp.float32)
    identity = (
        zero_vector,
        jnp.broadcast_to(jnp.eye(width, dtype=jnp.float32), (lines_here, width, width)),
    )
    local_forward = sweep_down(right_side, inverse_blocks, lower_blocks, zero_vector)
    down_total = None
    for cell in range(cells_here):
        factor = -block_times(
            inverse_blocks[cell].astype(jnp.float32), lower_blocks[cell].astype(jnp.float32)
        )
        down_total = factor if cell == 0 else block_times(factor, down_total)
    entering, _ = entering_2((local_forward[-1], down_total), "wall", compose_maps, identity, False)
    forward = sweep_down(right_side, inverse_blocks, lower_blocks, entering)
    local_back = sweep_up(forward, inverse_blocks, upper_blocks, zero_vector)
    up_total = None
    for cell in range(cells_here - 1, -1, -1):
        factor = -block_times(
            inverse_blocks[cell].astype(jnp.float32), upper_blocks[cell].astype(jnp.float32)
        )
        up_total = factor if cell == cells_here - 1 else block_times(factor, up_total)
    arriving, _ = entering_2((local_back[0], up_total), "wall", compose_maps, identity, True)
    correction = sweep_up(forward, inverse_blocks, upper_blocks, arriving)
    traces = jnp.einsum(
        "cld,df->clf", correction, trace_map.astype(jnp.float32), precision=lax.Precision.HIGHEST
    )
    total_lines = lines_here * lax.axis_size("tang")
    window = with_halo(traces, (("tang", 1),), lines_here)
    offset = (lax.axis_index("tang") - 1) * lines_here
    local_index = jnp.mod(neighbours - offset, total_lines)
    span = window.shape[1]
    facevars = traces.shape[2] // 4
    positions = jnp.arange(span, dtype=jnp.int32)
    pieces_list = []
    for face in range(4):
        other = face ^ 1
        selector = (local_index[:, face][:, None] == positions[None, :]).astype(jnp.float32)
        across = jnp.einsum(
            "gs,osp->ogp",
            selector,
            window[:, :, other * facevars : (other + 1) * facevars],
            precision=lax.Precision.HIGHEST,
        )
        pieces_list.append(traces[:, :, face * facevars : (face + 1) * facevars] - across)
    jump = jnp.concatenate(pieces_list, axis=2)
    face_residual = jnp.einsum(
        "clf,fd->cld", jump, lift_map.astype(jnp.float32), precision=lax.Precision.HIGHEST
    )
    return (correction, face_residual)


def solution(mesh):
    in_specs = (
        P("wall", "tang", None),
        P("wall", "tang", None, None),
        P("wall", "tang", None, None),
        P("wall", "tang", None, None),
        P(),
        P(),
        P("tang", None),
    )
    out_specs = (P("wall", "tang", None), P("wall", "tang", None))
    return jax.shard_map(body, mesh=mesh, in_specs=in_specs, out_specs=out_specs, check_vma=False)
```

profile of v0, /device:TPU:30, one launch (start us, length us, event | category | flops | bytes accessed | tf_op | source)
XLA Modules:
  0.0 517.6 jit_solution(18093461782852915793)
XLA Ops:
  9.7 3.4 fusion.138
  15.4 3.4 fusion.139
  22.1 36.5 %all-gather.4 = f32[16,2,384]{2,1,0:T(2,128)S(1)} all-gather(f32[1,2,384]{2,1,0:T(2,128)S(1)} %bitcast.236), channel_id=2, replica_groups=mesh['wall'=16,'tang'=32] {'wall'}, dimensions={0}, use_global_device_ids=true | all-gather | bytes 52224 | tf_op jit(solution)/shard_map/all_gather | solution.py:11
  59.2 174.2 %all-gather.9.cloned.1.call-done = f32[32,384,384]{2,1,0:T(8,128)} async-done(((f32[2,384,384]{2,1,0:T(8,128)}), f32[32,384,384]{2,1,0:T(8,128)}) %all-gather.9.cloned.1.call-update) | async-done | bytes 18874384 | tf_op jit(solution)/shard_map/all_gather | solution.py:11
  237.1 60.9 %all-gather.5 = f32[16,2,384]{2,1,0:T(2,128)S(1)} all-gather(f32[1,2,384]{2,1,0:T(2,128)S(1)} %fusion.94), channel_id=4, replica_groups=mesh['wall'=16,'tang'=32] {'wall'}, dimensions={0}, use_global_device_ids=true | all-gather | bytes 52224 | tf_op jit(solution)/shard_map/all_gather | solution.py:11
  298.0 147.5 %all-gather.11.cloned.1.call-done = f32[32,384,384]{2,1,0:T(8,128)} async-done(((f32[2,384,384]{2,1,0:T(8,128)}), f32[32,384,384]{2,1,0:T(8,128)}) %all-gather.11.cloned.1.call-update) | async-done | bytes 18874384 | tf_op jit(solution)/shard_map/all_gather | solution.py:11
  445.5 37.0 %while.27 = (s32[]{:T(128)}, f32[2,384]{1,0:T(2,128)S(1)}, s32[]{:T(128)}, f32[16,2,384]{2,1,0:T(2,128)S(1)}, f32[16,2,384,384]{3,2,1,0:T(8,128)}, /*index=5*/s32[]{:T(128)}, s32[]{:T(128)}, s32[]{:T(128)}, s32[]{:T(128)}) while((s32[]{:T(128)}, f32[2,384]{1,0:T(2,128)S(1)}, s32[]{:T(128)}, f32[16,2,384]{2,1,0:T(2,128)S(1)}, ...), condition=%wide.region_3.4_spmd, body=%wide.region_2.3_spmd.sunk | while | flops 3539718 | bytes 1195155 | solution.py:20
  445.5 2.5 fusion.156
  448.1 2.5 fusion.156
  450.5 2.5 fusion.156
  453.0 2.5 fusion.156
  455.4 2.5 fusion.156
  457.9 2.5 fusion.156
  460.4 2.5 fusion.156
  462.8 2.5 fusion.156
  465.3 2.5 fusion.156
  467.7 2.5 fusion.156
  470.2 2.5 fusion.156
  472.7 2.5 fusion.156
  475.1 2.5 fusion.156
  477.6 2.5 fusion.156
  480.0 2.5 fusion.156
  485.3 5.2 %collective-permute-start = (f32[2,2,384]{2,1,0:T(2,128)S(1)}, f32[2,2,384]{2,1,0:T(2,128)S(1)}, u32[]{:S(2)}, u32[]{:S(2)}) collective-permute-start(f32[2,2,384]{2,1,0:T(2,128)S(1)} %fusion.68), channel_id=1, source_target_pairs={{0,1},{1,2},{2,3},{3,4},{4,5},{5,6},{6,7},{7,8},{8,9},{9,10},{10,1... | collective-permute-start | bytes 18440 | tf_op jit(solution)/shard_map/ppermute | solution.py:30
  492.7 16.3 %collective-permute-done.1 = f32[2,2,384]{2,1,0:T(2,128)S(1)} collective-permute-done((f32[2,2,384]{2,1,0:T(2,128)S(1)}, f32[2,2,384]{2,1,0:T(2,128)S(1)}, u32[]{:S(2)}, u32[]{:S(2)}) %collective-permute-start.1) | collective-permute-done | bytes 6176 | tf_op jit(solution)/shard_map/ppermute | solution.py:31
  (91 shorter events, 19.1 us)
Async XLA Ops:
  7.2 477.9 %copy-start = (bf16[384,384]{1,0:T(8,128)(2,1)S(1)}, bf16[384,384]{1,0:T(8,128)(2,1)}, u32[]{:S(2)}) copy-start(bf16[384,384]{1,0:T(8,128)(2,1)} %param.15) | copy-start | bytes 884740
  7.2 2.0 copy-start.1
  7.2 2.0 copy-start.2
  7.2 226.2 %all-gather.9.cloned.1.call-start = ((), (), s32[]{:S(2)}) async-start(), calls=%async_computation | async-start | bytes 20054016 | tf_op jit(solution)/shard_map/all_gather | solution.py:11
  13.2 432.4 %all-gather.11.cloned.1.call-start = ((), (), s32[]{:S(2)}) async-start(), calls=%async_computation.1 | async-start | bytes 20054016 | tf_op jit(solution)/shard_map/all_gather | solution.py:11
  13.2 1.7 copy-start.3
  18.9 0.7 copy-start.8
  18.9 2.5 copy-start.4
  19.6 39.0 %copy-start.10 = (s32[2,4]{1,0:T(2,128)S(1)}, s32[2,4]{1,0:T(2,128)}, u32[]{:S(2)}) copy-start(s32[2,4]{1,0:T(2,128)} %param.17) | copy-start | bytes 100
  233.4 2.5 copy-start.5
  445.5 37.0 %copy-start.6 = (bf16[2,2,384,384]{3,2,1,0:T(8,128)(2,1)S(1)}, bf16[2,2,384,384]{3,2,1,0:T(8,128)(2,1)}, u32[]{:S(2)}) copy-start(bf16[2,2,384,384]{3,2,1,0:T(8,128)(2,1)} %param.14) | copy-start | bytes 3538948
  483.1 26.7 %copy-start.7 = (bf16[384,384]{1,0:T(8,128)(2,1)S(1)}, bf16[384,384]{1,0:T(8,128)(2,1)}, u32[]{:S(2)}) copy-start(bf16[384,384]{1,0:T(8,128)(2,1)} %param.16) | copy-start | bytes 884740
  485.1 25.7 %copy-start.9 = (f32[2,2,384]{2,1,0:T(2,128)}, f32[2,2,384]{2,1,0:T(2,128)S(1)}, u32[]{:S(2)}) copy-start(f32[2,2,384]{2,1,0:T(2,128)S(1)} %pad_maximum_fusion.1) | copy-start | bytes 18436
  485.3 7.4 %collective-permute-start = (f32[2,2,384]{2,1,0:T(2,128)S(1)}, f32[2,2,384]{2,1,0:T(2,128)S(1)}, u32[]{:S(2)}, u32[]{:S(2)}) collective-permute-start(f32[2,2,384]{2,1,0:T(2,128)S(1)} %fusion.68), channel_id=1, source_target_pairs={{0,1},{1,2},{2,3},{3,4},{4,5},{5,6},{6,7},{7,8},{8,9},{9,10},{10,1... | collective-permute-start | bytes 18440 | tf_op jit(solution)/shard_map/ppermute | solution.py:30
  490.6 18.5 %collective-permute-start.1 = (f32[2,2,384]{2,1,0:T(2,128)S(1)}, f32[2,2,384]{2,1,0:T(2,128)S(1)}, u32[]{:S(2)}, u32[]{:S(2)}) collective-permute-start(f32[2,2,384]{2,1,0:T(2,128)S(1)} %fusion.68), channel_id=1, source_target_pairs={{1,0},{2,1},{3,2},{4,3},{5,4},{6,5},{7,6},{8,7},{9,8},{10,9},{11,1... | collective-permute-start | bytes 18440 | tf_op jit(solution)/shard_map/ppermute | solution.py:31
Sparse Core Ops, SparseCore 0:
  13.3 220.0 all-gather.8
  235.5 210.0 all-gather.10
where the time goes:
time: 518 us
  waiting for transfers between devices  338 us (65%)
  blocking collectives  97.4 us (19%)
  matrix products  60.1 us (12%)
  between operations  14.2 us (3%)
  starting transfers between devices  7.23 us (1%)
    all_gather x2, waiting for transfers between devices, entering_2(): gathered = jax.tree.map(lambda a: lax.all_gather(a, axis), part)  322 us
    all_gather x2, blocking collectives, entering_2(): gathered = jax.tree.map(lambda a: lax.all_gather(a, axis), part)  97.4 us
    dot_general x31, matrix products, apply_block(): jnp.einsum('lij,lj->li', matrix.astype(jnp.float32), vector, precision=la...  46.7 us
    ppermute x1, waiting for transfers between devices, with_halo(): after = lax.ppermute(first, axis, down)  16.3 us
    dot_general x6, matrix products, block_times(): jnp.einsum('lij,ljm->lim', left, right, precision=lax.Precision.HIGHEST)  11.4 us
  transfers between devices with their start and end apart: 4, of which 3 were waited for; matrix products, arithmetic and copies ran while one was open for 3% of the time, Pallas kernels for 0%

commit v1 on v0

v1 whole, which is shorter than its diff:
```python
import jax
import jax.numpy as jnp
from jax import lax
from jax.experimental import pallas as pl
from jax.experimental.pallas import tpu as pltpu
from jax.sharding import PartitionSpec as P

F32 = jnp.float32
BF16 = jnp.bfloat16
NN = (((1,), (0,)), ((), ()))
NT = (((1,), (1,)), ((), ()))
VMEM = pl.BlockSpec(memory_space=pltpu.VMEM)
SMEM = pl.BlockSpec(memory_space=pltpu.SMEM)
LIMIT = 40 * 1024 * 1024


def dot(a, b, dims=NN):
    return lax.dot_general(a, b, dims, preferred_element_type=F32)


def split(x):
    high = x.astype(BF16)
    return high, (x - high.astype(F32)).astype(BF16)


def product(a, b):
    a_high, a_low = split(a)
    b_high, b_low = split(b)
    return dot(a_high, b_high) + dot(a_high, b_low) + dot(a_low, b_high)


def stacked(row):
    high, low = split(row)
    index = lax.broadcasted_iota(jnp.int32, (16, row.shape[1]), 0)
    zero = jnp.zeros((16, row.shape[1]), F32)
    high = jnp.broadcast_to(high.astype(F32), zero.shape)
    low = jnp.broadcast_to(low.astype(F32), zero.shape)
    return jnp.where(index == 0, high, jnp.where(index == 1, low, zero)).astype(BF16)


def apply_exact(block, row):
    out = dot(stacked(row), block, NT)
    return out[0:1] + out[1:2]


def apply_pair(pair, row):
    n = pair.shape[0] // 2
    out = dot(stacked(row), pair, NT)
    return out[0:1, :n] + out[1:2, :n] + out[0:1, n:]


def apply_full(matrix, row):
    high, low = split(matrix)
    rows = stacked(row)
    main = dot(rows, high, NT)
    rest = dot(rows, low, NT)
    return main[0:1] + main[1:2] + rest[0:1]


def put_pair(ref, matrix):
    n = matrix.shape[0]
    high, low = split(matrix)
    ref[0:n] = high
    ref[n:] = low


def put_row(ref, row):
    ref[...] = jnp.broadcast_to(row, ref.shape)


def call(kernel, outs, *args, scalars=0, flops=0, name=None):
    return pl.pallas_call(
        kernel,
        out_shape=[jax.ShapeDtypeStruct(s, t) for s, t in outs],
        in_specs=[SMEM] * scalars + [VMEM] * (len(args) - scalars),
        out_specs=[VMEM] * len(outs),
        compiler_params=pltpu.CompilerParams(vmem_limit_bytes=LIMIT),
        cost_estimate=pl.CostEstimate(flops=flops, bytes_accessed=0, transcendentals=0),
        name=name,
    )(*args)


def down_kernel(core, a, l, r, give, keep):
    n = a.shape[2]

    def one(i, _):
        line = jnp.where(i == 0, 1 - core[0], core[0])
        first = dot(a[0, line], l[0, line])
        second = dot(a[1, line], l[1, line])
        total = product(second, first)
        x = apply_exact(a[0, line], r[line, 0:1])
        x = apply_exact(a[1, line], r[line, 1:2] - apply_exact(l[1, line], x))

        @pl.when(i == 0)
        def _():
            give[0:n] = total
            give[n:] = jnp.broadcast_to(x, (8, n))

        @pl.when(i == 1)
        def _():
            keep[0:n] = total
            keep[n:] = jnp.broadcast_to(x, (8, n))

        return 0

    lax.fori_loop(0, 2, one, 0)


def up_kernel(core, a, l, u, r, give_f, keep_f, give, keep):
    n = a.shape[2]

    def one(i, _):
        line = jnp.where(i == 0, 1 - core[0], core[0])
        first = dot(a[0, line], u[0, line])
        second = dot(a[1, line], u[1, line])
        back = product(first, second)
        own = dot(a[0, line], l[0, line])
        x = apply_exact(a[0, line], r[line, 0:1])

        def finish(out, f):
            out[0:n] = back
            out[n : 2 * n] = -(own + product(first, f[0:n]))
            b = x - apply_exact(a[0, line], apply_exact(u[0, line], f[n : n + 1]))
            out[2 * n :] = jnp.broadcast_to(b, (8, n))

        @pl.when(i == 0)
        def _():
            finish(give, give_f)

        @pl.when(i == 1)
        def _():
            finish(keep, keep_f)

        return 0

    lax.fori_loop(0, 2, one, 0)


def down_join_kernel(core, got, keep, total, lower, vectors):
    n = got.shape[1]

    def finish(low, high):
        put_pair(total, product(high[0:n], low[0:n]))
        put_pair(lower, low[0:n])
        a = low[n : n + 1]
        vectors[0] = jnp.broadcast_to(high[n : n + 1] + apply_full(high[0:n], a), (8, n))
        vectors[1] = jnp.broadcast_to(a, (8, n))

    @pl.when(core[0] == 0)
    def _():
        finish(keep, got)

    @pl.when(core[0] == 1)
    def _():
        finish(got, keep)


def up_join_kernel(core, got, keep, total, b_low, b_high, g_low, g_high, vectors):
    n = got.shape[1]

    def finish(low, high):
        put_pair(total, product(low[0:n], high[0:n]))
        put_pair(b_low, low[0:n])
        put_pair(b_high, high[0:n])
        put_pair(g_low, low[n : 2 * n])
        put_pair(g_high, high[n : 2 * n])
        vectors[0] = low[2 * n :]
        vectors[1] = high[2 * n :]

    @pl.when(core[0] == 0)
    def _():
        finish(keep, got)

    @pl.when(core[0] == 1)
    def _():
        finish(got, keep)


def step_kernel(came, constant, pair, out):
    put_row(out, constant[0:1] + apply_pair(pair[...], came[0:1]))


def turn_kernel(core, e, f_vectors, lower, b_vectors, b_low, g_low, g_high, b_chip, b_up, give, keep):
    enter = e[0:1]
    middle = f_vectors[1, 0:1] + apply_pair(lower[...], enter)
    up = b_vectors[1, 0:1] + apply_pair(g_high[...], middle)
    low = b_vectors[0, 0:1] + apply_pair(g_low[...], enter)
    put_row(b_chip, low + apply_pair(b_low[...], up))
    put_row(b_up, up)
    first = core[0] == 0
    put_row(give, jnp.where(first, middle, enter))
    put_row(keep, jnp.where(first, enter, middle))


def local_kernel(core, r, a, l, u, got, keep, f):
    for line in range(2):
        mine = core[0] == line
        enter = jnp.where(mine, keep[0:1], got[0:1])
        one = apply_exact(a[0, line], r[line, 0:1] - apply_exact(l[0, line], enter))
        two = apply_exact(a[1, line], r[line, 1:2] - apply_exact(l[1, line], one))
        f[line, 0:1] = one
        f[line, 1:2] = two


def middle_kernel(core, c, b_up, b_high, give, keep):
    enter = c[0:1]
    middle = b_up[0:1] + apply_pair(b_high[...], enter)
    first = core[0] == 0
    put_row(give, jnp.where(first, enter, middle))
    put_row(keep, jnp.where(first, middle, enter))


def rows_exact(block, rows):
    m = rows.shape[0]
    high, low = split(rows)
    return dot(high, block) + dot(low, block)


def last_kernel(core, got, keep, f, a, u, w, correction, traces):
    n = w.shape[0]
    parts = [[None, None], [None, None]]
    for line in range(2):
        mine = core[0] == line
        enter = jnp.where(mine, keep[0:1], got[0:1])
        two = f[line, 1:2] - apply_exact(a[1, line], apply_exact(u[1, line], enter))
        one = f[line, 0:1] - apply_exact(a[0, line], apply_exact(u[0, line], two))
        parts[0][line] = one
        parts[1][line] = two
    index = lax.broadcasted_iota(jnp.int32, (16, n), 0)
    rows = jnp.zeros((16, n), F32)
    for cell in range(2):
        for line in range(2):
            row = parts[cell][line]
            correction[cell, line : line + 1] = row
            rows = jnp.where(index == cell * 2 + line, jnp.broadcast_to(row, (16, n)), rows)
    traces[...] = rows_exact(w[...], rows)[0:8]


def jump_kernel(traces, one, other, weights, lift, residual):
    n = lift.shape[0]
    own = traces[:, 0:n]
    mine = traces[:, n:]
    index = lax.broadcasted_iota(jnp.int32, (16, n), 0)
    rows = jnp.zeros((16, n), F32)
    for cell in range(2):
        for line in range(2):
            at = cell * 2 + line
            jump = own[at : at + 1]
            for side, source in enumerate((mine, one[...], other[...])):
                for k in range(2):
                    j = cell * 2 + k
                    jump = jump - weights[line, side * 2 + k : side * 2 + k + 1] * source[j : j + 1]
            rows = jnp.where(index == at, jnp.broadcast_to(jump, (16, n)), rows)
    out = rows_exact(lift[...], rows)
    for cell in range(2):
        residual[cell] = out[cell * 2 : cell * 2 + 2]


def body(right_side, inverse_blocks, lower_blocks, upper_blocks, trace_map, lift_map, neighbours):
    n = right_side.shape[2]
    wall, tang = lax.axis_size("wall"), lax.axis_size("tang")
    chips = wall // 2
    core = lax.rem(lax.axis_index("wall"), 2)
    scalar = jnp.reshape(core, (1,))
    r = jnp.transpose(right_side, (1, 0, 2))
    across = [(i, i ^ 1) for i in range(wall)]
    row = ((8, n), F32)
    pair = ((2 * n, n), BF16)

    here = lax.axis_index("tang")
    even = lax.rem(here, 2) == 0
    after, before = lax.rem(here + 1, tang), lax.rem(here + tang - 1, tang)
    near, far = jnp.where(even, after, before), jnp.where(even, before, after)
    places = jnp.stack([2 * here, 2 * here + 1, 2 * near, 2 * near + 1, 2 * far, 2 * far + 1])
    weights = (neighbours[:, None, :] == places[None, :, None]).astype(F32)
    weights = jnp.repeat(weights, n // 4, axis=2)
    face = trace_map.reshape(n, 4, n // 4)
    swapped = jnp.stack([face[:, 1], face[:, 0], face[:, 3], face[:, 2]], axis=1).reshape(n, n)
    both = jnp.concatenate([trace_map, swapped], axis=1)

    mul = 2 * n * n * n
    give_f, keep_f = call(
        down_kernel, [((n + 8, n), F32)] * 2, scalar, inverse_blocks, lower_blocks, r,
        scalars=1, flops=10 * mul, name="down",
    )
    got_f = lax.ppermute(give_f, "wall", across)
    give_b, keep_b = call(
        up_kernel, [((2 * n + 8, n), F32)] * 2,
        scalar, inverse_blocks, lower_blocks, upper_blocks, r, give_f, keep_f,
        scalars=1, flops=18 * mul, name="up",
    )
    total, lower, f_vectors = call(
        down_join_kernel, [pair, pair, ((2, 8, n), F32)], scalar, got_f, keep_f,
        scalars=1, flops=3 * mul, name="down_join",
    )
    got_b = lax.ppermute(give_b, "wall", across)
    back, b_low, b_high, g_low, g_high, b_vectors = call(
        up_join_kernel, [pair] * 5 + [((2, 8, n), F32)], scalar, got_b, keep_b,
        scalars=1, flops=3 * mul, name="up_join",
    )

    enter = jnp.zeros((8, n), F32)
    out = f_vectors[0]
    for chip in range(chips - 1):
        came = lax.ppermute(out, "wall", [(2 * chip + c, 2 * chip + 2 + c) for c in range(2)])
        enter = enter + came
        if chip < chips - 2:
            (out,) = call(step_kernel, [row], came, f_vectors[0], total, flops=mul // 100, name="step")

    b_chip, b_up, give, keep = call(
        turn_kernel, [row] * 4,
        scalar, enter, f_vectors, lower, b_vectors, b_low, g_low, g_high,
        scalars=1, flops=mul // 50, name="turn",
    )
    got = lax.ppermute(give, "wall", across)
    (forward,) = call(
        local_kernel, [((2, 2, n), F32)],
        scalar, r, inverse_blocks, lower_blocks, upper_blocks, got, keep,
        scalars=1, flops=mul // 20, name="local",
    )

    arrive = jnp.zeros((8, n), F32)
    out = b_chip
    for chip in range(chips - 1, 0, -1):
        came = lax.ppermute(out, "wall", [(2 * chip + c, 2 * chip - 2 + c) for c in range(2)])
        arrive = arrive + came
        if chip > 1:
            (out,) = call(step_kernel, [row], came, b_chip, back, flops=mul // 100, name="step")

    give, keep = call(
        middle_kernel, [row] * 2, scalar, arrive, b_up, b_high, scalars=1, flops=mul // 100, name="middle"
    )
    got = lax.ppermute(give, "wall", across)
    correction, traces = call(
        last_kernel, [((2, 2, n), F32), ((8, 2 * n), F32)],
        scalar, got, keep, forward, inverse_blocks, upper_blocks, both,
        scalars=1, flops=mul // 20, name="last",
    )
    sent = traces[:, n:]
    first = [(i, i + 1) for i in range(0, tang, 2)]
    second = [(i, (i + 1) % tang) for i in range(1, tang, 2)]
    from_far = lax.ppermute(sent, "tang", second + [(j, i) for i, j in second])
    from_near = lax.ppermute(sent, "tang", first + [(j, i) for i, j in first])
    (residual,) = call(
        jump_kernel, [((2, 2, n), F32)], traces, from_near, from_far, weights, lift_map,
        flops=mul // 50, name="jump",
    )
    return correction, residual


def solution(mesh):
    in_specs = (
        P("wall", "tang", None),
        P("wall", "tang", None, None),
        P("wall", "tang", None, None),
        P("wall", "tang", None, None),
        P(),
        P(),
        P("tang", None),
    )
    out_specs = (P("wall", "tang", None), P("wall", "tang", None))
    return jax.shard_map(body, mesh=mesh, in_specs=in_specs, out_specs=out_specs, check_vma=False)
```

time: 518 us -> 117 us (0.23)
  the two profiles are of different devices: /device:TPU:30 before, /device:TPU:1 now
where the time goes in v1:
time: 117 us
  starting transfers between devices  57.2 us (49%)
  waiting for transfers between devices  33 us (28%)
  Pallas kernels  17.7 us (15%)
  local copies, waits for them, and re-layouts  5.99 us (5%)
  between operations  1.44 us (1%)
  other arithmetic  1.24 us (1%)
    ppermute x7, waiting for transfers between devices, body(): lax.ppermute(out, 'wall', [(2 * chip + c, 2 * chip - 2 + c) for c in rang...  29.4 us
    pallas_call x21, Pallas kernels, call(): pl.pallas_call(kernel, out_shape=[jax.ShapeDtypeStruct(s, t) for s, t in...  17.7 us
    ppermute x1, starting transfers between devices, body(): from_far = lax.ppermute(sent, 'tang', second + [(j, i) for i, j in second])  16.9 us
    ppermute x2, starting transfers between devices, body(): got = lax.ppermute(give, 'wall', across)  16.8 us
    ppermute x1, starting transfers between devices, body(): got_b = lax.ppermute(give_b, 'wall', across)  8.78 us
    ppermute x7, starting transfers between devices, body(): lax.ppermute(out, 'wall', [(2 * chip + c, 2 * chip - 2 + c) for c in rang...  5.46 us
    ppermute x7, starting transfers between devices, body(): lax.ppermute(out, 'wall', [(2 * chip + c, 2 * chip + 2 + c) for c in rang...  5.43 us
    unnamed x18, local copies, waits for them, and re-layouts  4.78 us
  transfers between devices with their start and end apart: 20, of which 4 were waited for; matrix products, arithmetic and copies ran while one was open for 2% of the time, Pallas kernels for 3%

profile of v1, /device:TPU:1, one launch (start us, length us, event | category | flops | bytes accessed | tf_op | source)
XLA Modules:
  0.0 116.6 jit_solution(9868967197158681404)
XLA Ops:
  1.3 1.3 %copy-done = bf16[2,2,384,384]{3,2,1,0:T(8,128)(2,1)S(1)} copy-done((bf16[2,2,384,384]{3,2,1,0:T(8,128)(2,1)S(1)}, bf16[2,2,384,384]{3,2,1,0:T(8,128)(2,1)}, u32[]{:S(2)}) %copy-start) | copy-done | bytes 1179672
  2.6 1.3 %copy-done.3 = bf16[2,2,384,384]{3,2,1,0:T(8,128)(2,1)S(1)} copy-done((bf16[2,2,384,384]{3,2,1,0:T(8,128)(2,1)S(1)}, bf16[2,2,384,384]{3,2,1,0:T(8,128)(2,1)}, u32[]{:S(2)}) %copy-start.3) | copy-done | bytes 1179672
  3.9 3.0 %down.1 = (f32[392,384]{1,0:T(8,128)S(1)}, f32[392,384]{1,0:T(8,128)S(1)}) custom-call(s32[1]{0:T(128)} %bitcast.core, bf16[2,2,384,384]{3,2,1,0:T(8,128)(2,1)S(1)} %copy-done, bf16[2,2,384,384]{3,2,1,0:T(8,128)(2,1)S(1)} %copy-done.3, f32[2,2,384]{2,1,0:T(2,128)S(1)} %bitcast.16), custom_call_target="tpu_custom_call" | custom-call | flops 1132462080 | tf_op jit(solution)/shard_map/down/pallas_call | solution.py:72
  6.8 4.7 %up.1 = (f32[776,384]{1,0:T(8,128)S(1)}, f32[776,384]{1,0:T(8,128)S(1)}) custom-call(s32[1]{0:T(128)} %bitcast.core, bf16[2,2,384,384]{3,2,1,0:T(8,128)(2,1)S(1)} %copy-done, bf16[2,2,384,384]{3,2,1,0:T(8,128)(2,1)S(1)} %copy-done.3, bf16[2,2,384,384]{3,2,1,0:T(8,128)(2,1)S(1)} %copy-done.2, f32[2,2,384]{2,1,0:T(2,128)S(1)} %bitcast.17, ...), custom_call_target="tpu_custom_call" | custom-call | flops 2038431744 | tf_op jit(solution)/shard_map/up/pallas_call | solution.py:72
  11.5 8.8 %collective-permute-start.8 = (f32[776,384]{1,0:T(8,128)S(1)}, f32[776,384]{1,0:T(8,128)S(1)}, u32[]{:S(2)}, u32[]{:S(2)}) collective-permute-start(f32[776,384]{1,0:T(8,128)S(1)} %get-tuple-element.28), channel_id=1, source_target_pairs={{0,32},{32,0},{64,96},{96,64},{128,160},{160,128},{192,224},{224,1... | collective-permute-start | bytes 3575816 | tf_op jit(solution)/shard_map/ppermute | solution.py:296
  20.3 1.9 %collective-permute-start = (f32[392,384]{1,0:T(8,128)S(1)}, f32[392,384]{1,0:T(8,128)S(1)}, u32[]{:S(2)}, u32[]{:S(2)}) collective-permute-start(f32[392,384]{1,0:T(8,128)S(1)} %get-tuple-element.23.give_f), channel_id=1, source_target_pairs={{0,32},{32,0},{64,96},{96,64},{128,160},{160,128},{192,224},{224,1... | collective-permute-start | bytes 1806344 | tf_op jit(solution)/shard_map/ppermute | solution.py:286
  22.2 2.0 %collective-permute-done.got = f32[392,384]{1,0:T(8,128)S(1)} collective-permute-done((f32[392,384]{1,0:T(8,128)S(1)}, f32[392,384]{1,0:T(8,128)S(1)}, u32[]{:S(2)}, u32[]{:S(2)}) %collective-permute-start) | collective-permute-done | bytes 602144 | tf_op jit(solution)/shard_map/ppermute | solution.py:286
  24.2 0.9 down_join.1
  25.2 1.3 %collective-permute-start.1 = (f32[8,384]{1,0:T(8,128)S(1)}, f32[8,384]{1,0:T(8,128)S(1)}, u32[]{:S(2)}, u32[]{:S(2)}) collective-permute-start(f32[8,384]{1,0:T(8,128)S(1)} %slice_bitcast_fusion.constant), channel_id=1, source_target_pairs={{0,64},{32,96},{1,65},{33,97},{2,66},{34,98},{3,67},{35,99},{4,68}... | collective-permute-start | bytes 36872 | tf_op jit(solution)/shard_map/ppermute | solution.py:305
  26.5 0.8 collective-permute-done.1.came
  33.1 1.4 %up_join.1 = (bf16[768,384]{1,0:T(8,128)(2,1)S(1)}, bf16[768,384]{1,0:T(8,128)(2,1)S(1)}, bf16[768,384]{1,0:T(8,128)(2,1)S(1)}, bf16[768,384]{1,0:T(8,128)(2,1)S...) custom-call(s32[1]{0:T(128)} %bitcast.core, f32[776,384]{1,0:T(8,128)S(1)} %collective-permute-done.8.got, ...), custom_call_target="tpu_custom_call" | custom-call | flops 339738624 | tf_op jit(solution)/shard_map/up_join/pallas_call | solution.py:72
  41.4 1.3 %collective-permute-start.15 = (f32[8,384]{1,0:T(8,128)S(1)}, f32[8,384]{1,0:T(8,128)S(1)}, u32[]{:S(2)}, u32[]{:S(2)}) collective-permute-start(f32[8,384]{1,0:T(8,128)S(1)} %step.23), channel_id=1, source_target_pairs={{64,0},{96,32},{65,1},{97,33},{66,2},{98,34},{67,3},{99,35},{68,4}... | collective-permute-start | bytes 36872 | tf_op jit(solution)/shard_map/ppermute | solution.py:325
  42.8 0.9 copy.12
  43.7 2.6 %collective-permute-start.17 = (f32[8,384]{1,0:T(8,128)S(1)}, f32[8,384]{1,0:T(8,128)S(1)}, u32[]{:S(2)}, u32[]{:S(2)}) collective-permute-start(f32[8,384]{1,0:T(8,128)S(1)} %get-tuple-element.40), channel_id=1, source_target_pairs={{0,32},{32,0},{64,96},{96,64},{128,160},{160,128},{192,224},{224,1... | collective-permute-start | bytes 36872 | tf_op jit(solution)/shard_map/ppermute | solution.py:315
  46.3 29.4 %collective-permute-done.15 = f32[8,384]{1,0:T(8,128)S(1)} collective-permute-done((f32[8,384]{1,0:T(8,128)S(1)}, f32[8,384]{1,0:T(8,128)S(1)}, u32[]{:S(2)}, u32[]{:S(2)}) %collective-permute-start.15) | collective-permute-done | bytes 12320 | tf_op jit(solution)/shard_map/ppermute | solution.py:325
  76.0 14.2 %collective-permute-start.16 = (f32[8,384]{1,0:T(8,128)S(1)}, f32[8,384]{1,0:T(8,128)S(1)}, u32[]{:S(2)}, u32[]{:S(2)}) collective-permute-start(f32[8,384]{1,0:T(8,128)S(1)} %get-tuple-element.38), channel_id=1, source_target_pairs={{0,32},{32,0},{64,96},{96,64},{128,160},{160,128},{192,224},{224,1... | collective-permute-start | bytes 36872 | tf_op jit(solution)/shard_map/ppermute | solution.py:333
  90.2 1.1 pad_maximum_fusion.w
  91.4 1.3 %copy-done.4 = bf16[2,2,384,384]{3,2,1,0:T(8,128)(2,1)S(1)} copy-done((bf16[2,2,384,384]{3,2,1,0:T(8,128)(2,1)S(1)}, bf16[2,2,384,384]{3,2,1,0:T(8,128)(2,1)}, u32[]{:S(2)}) %copy-start.4) | copy-done | bytes 1179672
  92.7 1.3 %local.1.f = f32[2,2,384]{2,1,0:T(2,128)S(1)} custom-call(s32[1]{0:T(128)} %bitcast.core, f32[2,2,384]{2,1,0:T(2,128)S(1)} %bitcast.18, bf16[2,2,384,384]{3,2,1,0:T(8,128)(2,1)S(1)} %copy-done.1, bf16[2,2,384,384]{3,2,1,0:T(8,128)(2,1)S(1)} %copy-done.4, bf16[2,2,384,384]{3,2,1,0:T(8,128)(2,1)S(1)} %copy-done.2, f32[8,384]{1,0:T(8,128)S(1)} %collective-permute-done.17.got, ...), custom_call_target="tpu_custom_call" | custom-call | flops 5662310 | tf_op jit(solution)/shard_map/local/pallas_call | solution.py:72
  94.0 1.9 %last.1 = (f32[2,2,384]{2,1,0:T(2,128)}, f32[8,768]{1,0:T(8,128)S(1)}) custom-call(s32[1]{0:T(128)} %bitcast.core, f32[8,384]{1,0:T(8,128)S(1)} %collective-permute-done.16.got, f32[8,384]{1,0:T(8,128)S(1)} %get-tuple-element.39.keep, f32[2,2,384]{2,1,0:T(2,128)S(1)} %local.1.f, bf16[2,2,384,384]{3,2,1,0:T(8,128)(2,1)S(1)} %copy-done.1, ...), custom_call_target="tpu_custom_call" | custom-call | flops 5662310 | tf_op jit(solution)/shard_map/last/pallas_call | solution.py:72
  95.9 1.9 %collective-permute-start.18 = (f32[8,384]{1,0:T(8,128)S(1)}, f32[8,384]{1,0:T(8,128)S(1)}, u32[]{:S(2)}, u32[]{:S(2)}) collective-permute-start(f32[8,384]{1,0:T(8,128)S(1)} %slice.29), channel_id=1, source_target_pairs={{0,1},{2,3},{4,5},{6,7},{8,9},{10,11},{12,13},{14,15},{16,17},{18,... | collective-permute-start | bytes 36872 | tf_op jit(solution)/shard_map/ppermute | solution.py:343
  97.8 16.9 %collective-permute-start.19 = (f32[8,384]{1,0:T(8,128)S(1)}, f32[8,384]{1,0:T(8,128)S(1)}, u32[]{:S(2)}, u32[]{:S(2)}) collective-permute-start(f32[8,384]{1,0:T(8,128)S(1)} %slice.29), channel_id=1, source_target_pairs={{1,2},{3,4},{5,6},{7,8},{9,10},{11,12},{13,14},{15,16},{17,18},{19... | collective-permute-start | bytes 36872 | tf_op jit(solution)/shard_map/ppermute | solution.py:342
  115.0 0.8 collective-permute-done.19.other
  115.8 0.8 jump.1
  (68 shorter events, 13.5 us)
Async XLA Ops:
  11.5 21.6 %collective-permute-start.8 = (f32[776,384]{1,0:T(8,128)S(1)}, f32[776,384]{1,0:T(8,128)S(1)}, u32[]{:S(2)}, u32[]{:S(2)}) collective-permute-start(f32[776,384]{1,0:T(8,128)S(1)} %get-tuple-element.28), channel_id=1, source_target_pairs={{0,32},{32,0},{64,96},{96,64},{128,160},{160,128},{192,224},{224,1... | collective-permute-start | bytes 3575816 | tf_op jit(solution)/shard_map/ppermute | solution.py:296
  20.3 3.9 %collective-permute-start = (f32[392,384]{1,0:T(8,128)S(1)}, f32[392,384]{1,0:T(8,128)S(1)}, u32[]{:S(2)}, u32[]{:S(2)}) collective-permute-start(f32[392,384]{1,0:T(8,128)S(1)} %get-tuple-element.23.give_f), channel_id=1, source_target_pairs={{0,32},{32,0},{64,96},{96,64},{128,160},{160,128},{192,224},{224,1... | collective-permute-start | bytes 1806344 | tf_op jit(solution)/shard_map/ppermute | solution.py:286
  25.2 2.1 %collective-permute-start.1 = (f32[8,384]{1,0:T(8,128)S(1)}, f32[8,384]{1,0:T(8,128)S(1)}, u32[]{:S(2)}, u32[]{:S(2)}) collective-permute-start(f32[8,384]{1,0:T(8,128)S(1)} %slice_bitcast_fusion.constant), channel_id=1, source_target_pairs={{0,64},{32,96},{1,65},{33,97},{2,66},{34,98},{3,67},{35,99},{4,68}... | collective-permute-start | bytes 36872 | tf_op jit(solution)/shard_map/ppermute | solution.py:305
  27.5 0.7 collective-permute-start.2
  28.5 0.7 collective-permute-start.3
  29.4 0.7 collective-permute-start.4
  30.4 0.7 collective-permute-start.5
  31.4 0.7 collective-permute-start.6
  32.3 0.7 collective-permute-start.7
  35.3 0.7 collective-permute-start.9
  36.0 3.9 %copy-start.6 = (bf16[384,384]{1,0:T(8,128)(2,1)S(1)}, bf16[384,384]{1,0:T(8,128)(2,1)}, u32[]{:S(2)}) copy-start(bf16[384,384]{1,0:T(8,128)(2,1)} %param.11) | copy-start | bytes 884740
  36.3 0.7 collective-permute-start.10
  37.2 0.7 collective-permute-start.11
  38.2 0.7 collective-permute-start.12
  39.2 0.9 collective-permute-start.13
  40.4 0.7 collective-permute-start.14
  41.4 34.3 %collective-permute-start.15 = (f32[8,384]{1,0:T(8,128)S(1)}, f32[8,384]{1,0:T(8,128)S(1)}, u32[]{:S(2)}, u32[]{:S(2)}) collective-permute-start(f32[8,384]{1,0:T(8,128)S(1)} %step.23), channel_id=1, source_target_pairs={{64,0},{96,32},{65,1},{97,33},{66,2},{98,34},{67,3},{99,35},{68,4}... | collective-permute-start | bytes 36872 | tf_op jit(solution)/shard_map/ppermute | solution.py:325
  42.8 48.6 %copy-start.1 = (bf16[2,2,384,384]{3,2,1,0:T(8,128)(2,1)S(1)}, bf16[2,2,384,384]{3,2,1,0:T(8,128)(2,1)}, u32[]{:S(2)}) copy-start(bf16[2,2,384,384]{3,2,1,0:T(8,128)(2,1)} %a.7) | copy-start | bytes 3538948
  43.7 47.7 %collective-permute-start.17 = (f32[8,384]{1,0:T(8,128)S(1)}, f32[8,384]{1,0:T(8,128)S(1)}, u32[]{:S(2)}, u32[]{:S(2)}) collective-permute-start(f32[8,384]{1,0:T(8,128)S(1)} %get-tuple-element.40), channel_id=1, source_target_pairs={{0,32},{32,0},{64,96},{96,64},{128,160},{160,128},{192,224},{224,1... | collective-permute-start | bytes 36872 | tf_op jit(solution)/shard_map/ppermute | solution.py:315
  76.0 18.0 %collective-permute-start.16 = (f32[8,384]{1,0:T(8,128)S(1)}, f32[8,384]{1,0:T(8,128)S(1)}, u32[]{:S(2)}, u32[]{:S(2)}) collective-permute-start(f32[8,384]{1,0:T(8,128)S(1)} %get-tuple-element.38), channel_id=1, source_target_pairs={{0,32},{32,0},{64,96},{96,64},{128,160},{160,128},{192,224},{224,1... | collective-permute-start | bytes 36872 | tf_op jit(solution)/shard_map/ppermute | solution.py:333
  94.0 20.8 %copy-start.7 = (s32[2,4]{1,0:T(2,128)S(1)}, s32[2,4]{1,0:T(2,128)}, u32[]{:S(2)}) copy-start(s32[2,4]{1,0:T(2,128)} %param.13) | copy-start | bytes 100
  94.0 21.8 %copy-start.5 = (bf16[384,384]{1,0:T(8,128)(2,1)S(1)}, bf16[384,384]{1,0:T(8,128)(2,1)}, u32[]{:S(2)}) copy-start(bf16[384,384]{1,0:T(8,128)(2,1)} %lift.1) | copy-start | bytes 884740
  95.9 19.1 %collective-permute-start.18 = (f32[8,384]{1,0:T(8,128)S(1)}, f32[8,384]{1,0:T(8,128)S(1)}, u32[]{:S(2)}, u32[]{:S(2)}) collective-permute-start(f32[8,384]{1,0:T(8,128)S(1)} %slice.29), channel_id=1, source_target_pairs={{0,1},{2,3},{4,5},{6,7},{8,9},{10,11},{12,13},{14,15},{16,17},{18,... | collective-permute-start | bytes 36872 | tf_op jit(solution)/shard_map/ppermute | solution.py:343
  97.8 18.0 %collective-permute-start.19 = (f32[8,384]{1,0:T(8,128)S(1)}, f32[8,384]{1,0:T(8,128)S(1)}, u32[]{:S(2)}, u32[]{:S(2)}) collective-permute-start(f32[8,384]{1,0:T(8,128)S(1)} %slice.29), channel_id=1, source_target_pairs={{1,2},{3,4},{5,6},{7,8},{9,10},{11,12},{13,14},{15,16},{17,18},{19... | collective-permute-start | bytes 36872 | tf_op jit(solution)/shard_map/ppermute | solution.py:342
  (4 other events, 6.8 us)

commit v2 on v1

v2 whole, which is shorter than its diff:
```python
import functools

import jax
import jax.numpy as jnp
from jax import lax
from jax.experimental import pallas as pl
from jax.experimental.pallas import tpu as pltpu
from jax.sharding import PartitionSpec as P

F32 = jnp.float32
BF16 = jnp.bfloat16
NN = (((1,), (0,)), ((), ()))
NT = (((1,), (1,)), ((), ()))
VMEM = pl.BlockSpec(memory_space=pltpu.VMEM)
HBM = pl.BlockSpec(memory_space=pltpu.HBM)
SMEM = pl.BlockSpec(memory_space=pltpu.SMEM)
LIMIT = 16 * 1024 * 1024
WHOLE = 48 * 1024 * 1024


def dot(a, b, dims=NN):
    return lax.dot_general(a, b, dims, preferred_element_type=F32)


def split(x):
    high = x.astype(BF16)
    return high, (x - high.astype(F32)).astype(BF16)


def product(a, b):
    a_high, a_low = split(a)
    b_high, b_low = split(b)
    return dot(a_high, b_high) + dot(a_high, b_low) + dot(a_low, b_high)


def stacked(row):
    high, low = split(row)
    index = lax.broadcasted_iota(jnp.int32, (16, row.shape[1]), 0)
    zero = jnp.zeros((16, row.shape[1]), F32)
    high = jnp.broadcast_to(high.astype(F32), zero.shape)
    low = jnp.broadcast_to(low.astype(F32), zero.shape)
    return jnp.where(index == 0, high, jnp.where(index == 1, low, zero)).astype(BF16)


def apply_exact(block, row):
    out = dot(stacked(row), block, NT)
    return out[0:1] + out[1:2]


def apply_pair(pair, row):
    n = pair.shape[0] // 2
    out = dot(stacked(row), pair, NT)
    return out[0:1, :n] + out[1:2, :n] + out[0:1, n:]


def apply_full(matrix, row):
    high, low = split(matrix)
    rows = stacked(row)
    main = dot(rows, high, NT)
    rest = dot(rows, low, NT)
    return main[0:1] + main[1:2] + rest[0:1]


def put_pair(ref, matrix):
    n = matrix.shape[0]
    high, low = split(matrix)
    ref[0:n] = high
    ref[n:] = low


def put_row(ref, row):
    ref[...] = jnp.broadcast_to(row, ref.shape)


def call(kernel, outs, *args, scalars=0, flops=0, name=None, after=()):
    count = len(args)
    operands = list(args) + list(after)

    def inner(*refs):
        kernel(*refs[:count], *refs[len(operands) :])

    return pl.pallas_call(
        inner,
        out_shape=[jax.ShapeDtypeStruct(s, t) for s, t in outs],
        in_specs=[SMEM] * scalars + [VMEM] * (len(operands) - scalars),
        out_specs=[VMEM] * len(outs),
        compiler_params=pltpu.CompilerParams(vmem_limit_bytes=LIMIT),
        cost_estimate=pl.CostEstimate(flops=flops, bytes_accessed=0, transcendentals=0),
        name=name,
    )(*operands)


def line_maps(a, l, u, r, out, ahead, back, rows):
    n = r[0].shape[1]
    a0, l0 = a(0), l(0)
    first = dot(a0, l0)
    x = apply_exact(a0, r[0])
    a1, l1 = a(1), l(1)
    up = product(dot(a1, l1), first)
    y = apply_exact(a1, r[1] - apply_exact(l1, x))
    u0 = u(0)
    near = dot(a0, u0)
    turn = -(first + product(near, up))
    x = x - apply_exact(a0, apply_exact(u0, y))
    far = dot(a1, u(1))
    down = product(near, far)
    out[0:n] = up
    out[n : 2 * n] = turn
    out[2 * n : 3 * n] = down
    index = lax.broadcasted_iota(jnp.int32, (8, n), 0)
    both = jnp.where(index == 0, jnp.broadcast_to(y, (8, n)), jnp.broadcast_to(x, (8, n)))
    out[3 * n :] = both
    rows[...] = both
    for ref, parts in ((ahead, (turn, up)), (back, (far, down))):
        for i, part in enumerate(parts):
            high, low = split(part)
            ref[i * n : (i + 1) * n] = high
            ref[(2 + i) * n : (3 + i) * n] = low


def first_kernel(line_ref, r, a, l, u, out, ahead, back, rows, r_here, a_here, l_here, u_here, sems):
    line = line_ref[0]
    copies = [pltpu.make_async_copy(r, r_here, sems.at[0])]
    for at in (line, 1 - line):
        for cell, source, here in (
            (0, a, a_here), (0, l, l_here), (1, a, a_here), (1, l, l_here), (0, u, u_here), (1, u, u_here)
        ):
            copies.append(pltpu.make_async_copy(source.at[cell, at], here.at[cell, at], sems.at[len(copies)]))
    for copy in copies:
        copy.start()

    def arrived(here, place):
        def get(cell):
            copies[place[cell]].wait()
            return here[cell, line]

        return get

    copies[0].wait()
    blocks = [arrived(a_here, (1, 3)), arrived(l_here, (2, 4)), arrived(u_here, (5, 6))]
    line_maps(*blocks, [r_here[cell, pl.ds(line, 1), :] for cell in range(2)], out, ahead, back, rows)
    for copy in copies[7:]:
        copy.wait()


def second_kernel(line_ref, r, a, l, u, out, ahead, back, rows):
    line = line_ref[0]
    blocks = [lambda cell, here=here: here[cell, line] for here in (a, l, u)]
    line_maps(*blocks, [r[cell, pl.ds(line, 1), :] for cell in range(2)], out, ahead, back, rows)


def down_join_kernel(core, got, keep, chip, total, lower, a_chip, a_low):
    n = got.shape[1]

    def finish(low, high):
        matrix = product(high[0:n], low[0:n])
        put_pair(total, matrix)
        put_pair(lower, low[0:n])
        a = low[3 * n : 3 * n + 1]
        joined = high[3 * n : 3 * n + 1] + apply_full(high[0:n], a)
        chip[0:n] = matrix
        chip[n:] = jnp.broadcast_to(joined, (8, n))
        put_row(a_chip, joined)
        put_row(a_low, a)

    @pl.when(core[0] == 0)
    def _():
        finish(keep, got)

    @pl.when(core[0] == 1)
    def _():
        finish(got, keep)


def up_join_kernel(core, got, keep, chip, total, b_low, b_high, g_low, g_high, v_low, v_high):
    n = got.shape[1]

    def finish(low, high):
        matrix = product(low[2 * n : 3 * n], high[2 * n : 3 * n])
        chip[...] = matrix
        put_pair(total, matrix)
        put_pair(b_low, low[2 * n : 3 * n])
        put_pair(b_high, high[2 * n : 3 * n])
        put_pair(g_low, low[n : 2 * n])
        put_pair(g_high, high[n : 2 * n])
        put_row(v_low, low[3 * n + 1 : 3 * n + 2])
        put_row(v_high, high[3 * n + 1 : 3 * n + 2])

    @pl.when(core[0] == 0)
    def _():
        finish(keep, got)

    @pl.when(core[0] == 1)
    def _():
        finish(got, keep)


def pair_row_kernel(came, pair, row):
    n = came.shape[1]
    put_pair(pair, came[0:n])
    row[...] = came[n:]


def pair_kernel(came, pair, token):
    put_pair(pair, came[...])
    token[...] = jnp.zeros(token.shape, F32)


def total_of(refs):
    out = refs[0][0:1]
    for ref in refs[1:]:
        out = out + ref[0:1]
    return out


def step_kernel(constant, pair, *refs):
    *x, out = refs
    put_row(out, constant[0:1] + apply_pair(pair[...], total_of(x)))


def entering(before, y, x):
    return total_of(x) + apply_pair(before[...], total_of(y))


def jump_step_kernel(many, before, constant, pair, *refs):
    *x, out = refs
    put_row(out, constant[0:1] + apply_pair(pair[...], entering(before, x[:many], x[many:])))


def turn_kernel(many, before, a_low, lower, v_low, v_high, b_low, g_low, g_high, *refs):
    *x, b_chip = refs
    enter = entering(before, x[:many], x[many:])
    middle = a_low[0:1] + apply_pair(lower[...], enter)
    up = v_high[0:1] + apply_pair(g_high[...], middle)
    low = v_low[0:1] + apply_pair(g_low[...], enter)
    put_row(b_chip, low + apply_pair(b_low[...], up))


def spread_kernel(many, core, before, a_low, lower, v_high, g_high, *refs):
    *x, b_up, give, keep = refs
    enter = entering(before, x[:many], x[many:])
    middle = a_low[0:1] + apply_pair(lower[...], enter)
    put_row(b_up, v_high[0:1] + apply_pair(g_high[...], middle))
    first = core[0] == 0
    put_row(give, jnp.where(first, middle, enter))
    put_row(keep, jnp.where(first, enter, middle))


def local_kernel(size, core, here, near, give_map, keep_map, give_rows, keep_rows, got, keep, f, weights):
    n = got.shape[1]
    column = lax.broadcasted_iota(jnp.int32, (1, n), 1)
    at = here[0]
    up, down = lax.rem(at + 1, size), lax.rem(at + size - 1, size)
    even = lax.rem(at, 2) == 0
    sides = (at, jnp.where(even, up, down), jnp.where(even, down, up))
    places = [2 * side + k for side in sides for k in range(2)]
    for i, (maps, rows, enter) in enumerate(((give_map, give_rows, got), (keep_map, keep_rows, keep))):
        moved = apply_pair(maps[...], enter[0:1])
        f[i, 0:1] = rows[1:2] + moved[:, :n]
        f[i, 1:2] = rows[0:1] + moved[:, n:]
    for line in range(2):
        for k in range(6):
            row = jnp.zeros((1, n), F32)
            for face in range(4):
                inside = (column >= face * (n // 4)) & (column < (face + 1) * (n // 4))
                meets = near[line, face] == places[k]
                row = jnp.where(inside, jnp.where(meets, 1.0, 0.0), row)
            weights[line, k : k + 1] = row


def middle_kernel(many, core, before, b_up, b_high, *refs):
    *x, give, keep = refs
    enter = entering(before, x[:many], x[many:])
    middle = b_up[0:1] + apply_pair(b_high[...], enter)
    first = core[0] == 0
    put_row(give, jnp.where(first, enter, middle))
    put_row(keep, jnp.where(first, middle, enter))


def rows_exact(block, rows):
    high, low = split(rows)
    return dot(high, block) + dot(low, block)


def last_kernel(core, got, keep, f, give_map, keep_map, w, correction, own, sent):
    n = w.shape[0]
    values = []
    for i, (maps, enter) in enumerate(((give_map, got), (keep_map, keep))):
        moved = apply_pair(maps[...], enter[0:1])
        values.append((f[i, 0:1] + moved[:, n:], f[i, 1:2] - moved[:, :n]))
    index = lax.broadcasted_iota(jnp.int32, (16, n), 0)
    rows = jnp.zeros((16, n), F32)
    first = core[0] == 0
    for cell in range(2):
        given, own_row = values[0][cell], values[1][cell]
        for line, row in enumerate((jnp.where(first, own_row, given), jnp.where(first, given, own_row))):
            correction[cell, line : line + 1] = row
            rows = jnp.where(index == cell * 2 + line, jnp.broadcast_to(row, (16, n)), rows)
    traces = rows_exact(w[...], rows)[0:8]
    own[...] = traces
    width = n // 4
    column = lax.broadcasted_iota(jnp.int32, (8, n), 1)
    lower = (column < width) | ((column >= 2 * width) & (column < 3 * width))
    sent[...] = jnp.where(lower, pltpu.roll(traces, n - width, 1), pltpu.roll(traces, width, 1))


def jump_kernel(own, mine, one, other, weights, lift, residual):
    n = lift.shape[0]
    index = lax.broadcasted_iota(jnp.int32, (16, n), 0)
    rows = jnp.zeros((16, n), F32)
    for cell in range(2):
        for line in range(2):
            at = cell * 2 + line
            jump = own[at : at + 1]
            for side, source in enumerate((mine, one, other)):
                for k in range(2):
                    j = cell * 2 + k
                    jump = jump - weights[line, side * 2 + k : side * 2 + k + 1] * source[j : j + 1]
            rows = jnp.where(index == at, jnp.broadcast_to(jump, (16, n)), rows)
    out = rows_exact(lift[...], rows)
    for cell in range(2):
        residual[cell] = out[cell * 2 : cell * 2 + 2]


def chips_to(pairs):
    return [(2 * i + c, 2 * j + c) for i, j in pairs for c in range(2)]


def body(right_side, inverse_blocks, lower_blocks, upper_blocks, trace_map, lift_map, neighbours):
    n = right_side.shape[2]
    wall, tang = lax.axis_size("wall"), lax.axis_size("tang")
    chips = wall // 2
    jumps = chips // 4
    singles = chips - 2 * jumps
    core = lax.rem(lax.axis_index("wall"), 2)
    own_line = jnp.reshape(core, (1,))
    other_line = 1 - own_line
    r, a, l, u = right_side, inverse_blocks, lower_blocks, upper_blocks
    across = [(i, i ^ 1) for i in range(wall)]
    row = ((8, n), F32)
    pair = ((2 * n, n), BF16)
    joined = ((n + 8, n), F32)

    here = jnp.reshape(lax.axis_index("tang"), (1,))

    mul = 2 * n * n * n
    maps = [((3 * n + 8, n), F32), ((4 * n, n), BF16), ((4 * n, n), BF16), row]
    here_now = [(r.shape, F32)] + [(a.shape, BF16)] * 3
    give, give_ahead, give_back, give_rows, r, a, l, u = pl.pallas_call(
        first_kernel,
        out_shape=[jax.ShapeDtypeStruct(*x) for x in maps + here_now],
        in_specs=[SMEM] + [HBM] * 4,
        out_specs=[VMEM] * 8,
        scratch_shapes=[pltpu.SemaphoreType.DMA((13,))],
        compiler_params=pltpu.CompilerParams(vmem_limit_bytes=WHOLE),
        cost_estimate=pl.CostEstimate(flops=13 * mul, bytes_accessed=0, transcendentals=0),
        name="first",
    )(other_line, r, a, l, u)
    got = lax.ppermute(give, "wall", across)
    keep, keep_ahead, keep_back, keep_rows = call(
        second_kernel, maps, own_line, r, a, l, u, scalars=1, flops=13 * mul, name="second"
    )
    chip_f, total, lower, a_chip, a_low = call(
        down_join_kernel, [joined, pair, pair, row, row], own_line, got, keep,
        scalars=1, flops=3 * mul, name="down_join",
    )
    chip_b, back, b_low, b_high, g_low, g_high, v_low, v_high = call(
        up_join_kernel, [((n, n), F32)] + [pair] * 5 + [row] * 2, own_line, got, keep,
        scalars=1, flops=3 * mul, name="up_join", after=(a_chip,),
    )
    moved_b = lax.ppermute(chip_b, "wall", chips_to([(k, k - 1) for k in range(chips - 2, 0, -2)]))

    moved_f = lax.ppermute(
        chip_f, "wall", chips_to([(k, k + 1) for k in range(singles, chips, 2)])
    )
    x, y = [], []
    out = a_chip
    for k in range(1, singles):
        x.append(lax.ppermute(out, "wall", chips_to([(k - 1, k)])))
        (out,) = call(step_kernel, [row], a_chip, total, *x, flops=mul // 100, name="step")
    pre, pre_row = call(pair_row_kernel, [pair, row], moved_f, flops=mul // 10, name="pre")
    for k in range(jumps):
        last = singles + 2 * k - 1
        y.append(lax.ppermute(out, "wall", chips_to([(last, last + 2)])))
        if k == jumps - 1:
            side = lax.ppermute(
                out, "wall", chips_to([(singles + 2 * j - 1, singles + 2 * j) for j in range(jumps)])
            )
        else:
            (out,) = call(
                functools.partial(jump_step_kernel, k + 1), [row], pre, a_chip, total, *y, *x, pre_row,
                flops=mul // 50, name="jump_step",
            )
    x = [*x, side, pre_row]
    entry, token = call(pair_kernel, [pair, row], moved_b, flops=mul // 10, name="entry")
    (b_chip,) = call(
        functools.partial(turn_kernel, jumps), [row],
        pre, a_low, lower, v_low, v_high, b_low, g_low, g_high, *y, *x,
        flops=mul // 50, name="turn", after=(token,),
    )

    odd = list(range(chips - 1, 0, -2))
    z = []
    out = b_chip
    waits = ()
    for k in odd[1:]:
        z.append(lax.ppermute(out, "wall", chips_to([(k + 2, k)])))
        if len(z) == 1:
            sent = lax.ppermute(b_chip, "wall", chips_to([(j, j - 1) for j in range(chips - 2, 0, -2)]))
        if k == 1:
            done = out
            b_up, give, keep = call(
                functools.partial(spread_kernel, jumps), [row] * 3, own_line, pre, a_low, lower, v_high, g_high, *y, *x,
                scalars=1, flops=mul // 50, name="spread",
            )
            got = lax.ppermute(give, "wall", across)
            forward, weights = call(
                functools.partial(local_kernel, tang), [((2, 2, n), F32), ((2, 8, n), F32)],
            own_line, here, neighbours, give_ahead, keep_ahead, give_rows, keep_rows, got, keep,
                scalars=3, flops=mul // 20, name="local",
            )
            waits = (weights,)
        (out,) = call(
            functools.partial(jump_step_kernel, len(z)), [row], entry, b_chip, back, *z, sent,
            flops=mul // 50, name="back_step", after=waits,
        )
    ends = lax.ppermute(out, "wall", chips_to([(k, k - 1) for k in odd]))

    give, keep = call(
        functools.partial(middle_kernel, len(z)), [row] * 2, own_line, entry, b_up, b_high, *z, sent, ends,
        scalars=1, flops=mul // 100, name="middle", after=(forward,),
    )
    got = lax.ppermute(give, "wall", across)
    correction, traces, sent = call(
        last_kernel, [((2, 2, n), F32), row, row], own_line, got, keep, forward, give_back, keep_back, trace_map,
        scalars=1, flops=mul // 20, name="last",
    )
    first = [(i, i + 1) for i in range(0, tang, 2)]
    second = [(i, (i + 1) % tang) for i in range(1, tang, 2)]
    from_near = lax.ppermute(sent, "tang", first + [(j, i) for i, j in first])
    from_far = lax.ppermute(sent, "tang", second + [(j, i) for i, j in second])
    (residual,) = call(
        jump_kernel, [((2, 2, n), F32)], traces, sent, from_near, from_far, weights, lift_map,
        flops=mul // 50, name="jump",
    )
    return correction, residual


def solution(mesh):
    in_specs = (
        P("wall", "tang", None),
        P("wall", "tang", None, None),
        P("wall", "tang", None, None),
        P("wall", "tang", None, None),
        P(),
        P(),
        P("tang", None),
    )
    out_specs = (P("wall", "tang", None), P("wall", "tang", None))
    return jax.shard_map(body, mesh=mesh, in_specs=in_specs, out_specs=out_specs, check_vma=False)
```

time: 117 us -> 103 us (0.88)
  the two profiles are of different devices: /device:TPU:1 before, /device:TPU:64 now
where the time goes in v2:
time: 103 us; the launch traced here: 102 us
  starting transfers between devices  38.2 us (37%)
  waiting for transfers between devices  32.9 us (32%)
  Pallas kernels  23.6 us (23%)
  local copies, waits for them, and re-layouts  6.46 us (6%)
  between operations  1.32 us (1%)
    ppermute x1, waiting for transfers between devices, body(): ends = lax.ppermute(out, 'wall', chips_to([(k, k - 1) for k in odd]))  18.4 us
    pallas_call x18, Pallas kernels, call(): pl.pallas_call(inner, out_shape=[jax.ShapeDtypeStruct(s, t) for s, t in o...  17.1 us
    ppermute x1, starting transfers between devices, body(): from_far = lax.ppermute(sent, 'tang', second + [(j, i) for i, j in second])  15.5 us
    ppermute x3, waiting for transfers between devices, body(): x.append(lax.ppermute(out, 'wall', chips_to([(k - 1, k)])))  9.55 us
    pallas_call x1, Pallas kernels, body(): pl.pallas_call(first_kernel, out_shape=[jax.ShapeDtypeStruct(*x) for x in...  6.48 us
    unnamed x48, local copies, waits for them, and re-layouts  6.46 us
    ppermute x3, starting transfers between devices, body(): got = lax.ppermute(give, 'wall', across)  5.75 us
    ppermute x1, starting transfers between devices, body(): from_near = lax.ppermute(sent, 'tang', first + [(j, i) for i, j in first])  3.39 us
  transfers between devices with their start and end apart: 18, of which 6 were waited for; matrix products, arithmetic and copies ran while one was open for 0% of the time, Pallas kernels for 10%

profile of v2, /device:TPU:64, one launch (start us, length us, event | category | flops | bytes accessed | tf_op | source)
XLA Modules:
  0.0 102.4 jit_solution(3075037907631490121)
XLA Ops:
  1.3 6.5 %first.1 = (f32[1160,384]{1,0:T(8,128)}, bf16[1536,384]{1,0:T(8,128)(2,1)S(1)}, bf16[1536,384]{1,0:T(8,128)(2,1)S(1)}, f32[8,384]{1,0:T(8,128)S(1)}, f32[2,2,384...) custom-call(s32[1]{0:T(128)S(6)} %sub.3.line_ref, ...), custom_call_target="tpu_custom_call" | custom-call | flops 1472200704 | tf_op jit(solution)/shard_map/first/pallas_call | solution.py:349
  7.8 1.9 %collective-permute-start = (f32[1160,384]{1,0:T(8,128)}, f32[1160,384]{1,0:T(8,128)S(1)}, u32[]{:S(2)}, u32[]{:S(2)}) collective-permute-start(f32[1160,384]{1,0:T(8,128)} %get-tuple-element.41), channel_id=1, source_target_pairs={{0,32},{32,0},{64,96},{96,64},{128,160},{160,128},{192,224},{224,1... | collective-permute-start | bytes 5345288 | tf_op jit(solution)/shard_map/ppermute | solution.py:359
  9.8 3.5 %second.1 = (f32[1160,384]{1,0:T(8,128)S(1)}, bf16[1536,384]{1,0:T(8,128)(2,1)S(1)}, bf16[1536,384]{1,0:T(8,128)(2,1)S(1)}, f32[8,384]{1,0:T(8,128)S(1)}) custom-call(s32[1]{0:T(128)} %bitcast.refs_0_, f32[2,2,384]{2,1,0:T(2,128)S(1)} %get-tuple-element.42.refs_1_, bf16[2,2,384,384]{3,2,1,0:T(8,128)(2,1)S(1)} %get-tuple-element.43.refs_2_, ...), custom_call_target="tpu_custom_call" | custom-call | flops 1472200704 | tf_op jit(solution)/shard_map/second/pallas_call | solution.py:82
  16.0 1.4 %up_join.1 = (f32[384,384]{1,0:T(8,128)S(1)}, bf16[768,384]{1,0:T(8,128)(2,1)S(1)}, bf16[768,384]{1,0:T(8,128)(2,1)S(1)}, bf16[768,384]{1,0:T(8,128)(2,1)S(1)}, ...) custom-call(s32[1]{0:T(128)} %bitcast.refs_0_, ...), custom_call_target="tpu_custom_call" | custom-call | flops 339738624 | tf_op jit(solution)/shard_map/up_join/pallas_call | solution.py:82
  17.4 2.0 %collective-permute-start.1 = (f32[384,384]{1,0:T(8,128)S(1)}, f32[384,384]{1,0:T(8,128)S(1)}, u32[]{:S(2)}, u32[]{:S(2)}) collective-permute-start(f32[384,384]{1,0:T(8,128)S(1)} %get-tuple-element.48), channel_id=1, source_target_pairs={{384,320},{416,352},{256,192},{288,224},{128,64},{160,96},{385,321... | collective-permute-start | bytes 1769480 | tf_op jit(solution)/shard_map/ppermute | solution.py:371
  20.4 1.3 %collective-permute-start.4 = (f32[8,384]{1,0:T(8,128)S(1)}, f32[8,384]{1,0:T(8,128)S(1)}, u32[]{:S(2)}, u32[]{:S(2)}) collective-permute-start(f32[8,384]{1,0:T(8,128)S(1)} %step.3), channel_id=1, source_target_pairs={{64,128},{96,160},{65,129},{97,161},{66,130},{98,162},{67,131},{99... | collective-permute-start | bytes 36872 | tf_op jit(solution)/shard_map/ppermute | solution.py:379
  21.7 8.2 %collective-permute-done.4.refs_3_.refs_5_.refs_9_.refs_11_ = f32[8,384]{1,0:T(8,128)S(1)} collective-permute-done((f32[8,384]{1,0:T(8,128)S(1)}, f32[8,384]{1,0:T(8,128)S(1)}, u32[]{:S(2)}, u32[]{:S(2)}) %collective-permute-start.4) | collective-permute-done | bytes 12320 | tf_op jit(solution)/shard_map/ppermute | solution.py:379
  30.1 1.3 %collective-permute-start.5 = (f32[8,384]{1,0:T(8,128)S(1)}, f32[8,384]{1,0:T(8,128)S(1)}, u32[]{:S(2)}, u32[]{:S(2)}) collective-permute-start(f32[8,384]{1,0:T(8,128)S(1)} %step.4), channel_id=1, source_target_pairs={{128,192},{160,224},{129,193},{161,225},{130,194},{162,226},{131,1... | collective-permute-start | bytes 36872 | tf_op jit(solution)/shard_map/ppermute | solution.py:379
  31.5 1.4 %collective-permute-done.5.refs_4_.refs_6_.refs_10_.refs_12_ = f32[8,384]{1,0:T(8,128)S(1)} collective-permute-done((f32[8,384]{1,0:T(8,128)S(1)}, f32[8,384]{1,0:T(8,128)S(1)}, u32[]{:S(2)}, u32[]{:S(2)}) %collective-permute-start.5) | collective-permute-done | bytes 12320 | tf_op jit(solution)/shard_map/ppermute | solution.py:379
  37.2 1.3 %collective-permute-start.10 = (f32[8,384]{1,0:T(8,128)S(1)}, f32[8,384]{1,0:T(8,128)S(1)}, u32[]{:S(2)}, u32[]{:S(2)}) collective-permute-start(f32[8,384]{1,0:T(8,128)S(1)} %turn.1.refs_1_), channel_id=1, source_target_pairs={{384,320},{416,352},{256,192},{288,224},{128,64},{160,96},{385,321... | collective-permute-start | bytes 36872 | tf_op jit(solution)/shard_map/ppermute | solution.py:409
  41.3 1.2 %spread.1 = (f32[8,384]{1,0:T(8,128)S(1)}, f32[8,384]{1,0:T(8,128)}, f32[8,384]{1,0:T(8,128)S(1)}) custom-call(s32[1]{0:T(128)} %bitcast.refs_0_, bf16[768,384]{1,0:T(8,128)(2,1)S(1)} %get-tuple-element.51.refs_0_.refs_1_, f32[8,384]{1,0:T(8,128)S(1)} %get-tuple-element.52.refs_2_.refs_1_, bf16[768,384]{1,0:T(8,128)(2,1)S(1)} %get-tuple-element.53.refs_3_.refs_2_, ...), custom_call_target="tpu_custom_call" | custom-call | flops 2264924 | tf_op jit(solution)/shard_map/spread/pallas_call | solution.py:82
  42.5 1.9 %collective-permute-start.13 = (f32[8,384]{1,0:T(8,128)}, f32[8,384]{1,0:T(8,128)}, u32[]{:S(2)}, u32[]{:S(2)}) collective-permute-start(f32[8,384]{1,0:T(8,128)} %get-tuple-element.69), channel_id=1, source_target_pairs={{0,32},{32,0},{64,96},{96,64},{128,160},{160,128},{192,224},{224,1... | collective-permute-start | bytes 36872 | tf_op jit(solution)/shard_map/ppermute | solution.py:416
  45.6 1.3 %collective-permute-start.12 = (f32[8,384]{1,0:T(8,128)}, f32[8,384]{1,0:T(8,128)}, u32[]{:S(2)}, u32[]{:S(2)}) collective-permute-start(f32[8,384]{1,0:T(8,128)} %back_step.4), channel_id=1, source_target_pairs={{192,64},{224,96},{193,65},{225,97},{194,66},{226,98},{195,67},{22... | collective-permute-start | bytes 36872 | tf_op jit(solution)/shard_map/ppermute | solution.py:407
  46.8 1.3 %copy-done.1 = bf16[1536,384]{1,0:T(8,128)(2,1)S(1)} copy-done((bf16[1536,384]{1,0:T(8,128)(2,1)S(1)}, bf16[1536,384]{1,0:T(8,128)(2,1)}, u32[]{:S(2)}) %copy-start.1) | copy-done | bytes 1179672
  48.1 1.3 %copy-done.3 = bf16[1536,384]{1,0:T(8,128)(2,1)S(1)} copy-done((bf16[1536,384]{1,0:T(8,128)(2,1)S(1)}, bf16[1536,384]{1,0:T(8,128)(2,1)}, u32[]{:S(2)}) %copy-start.3) | copy-done | bytes 1179672
  51.5 1.5 %local.1 = (f32[2,2,384]{2,1,0:T(2,128)S(1)}, f32[2,8,384]{2,1,0:T(8,128)S(1)}) custom-call(s32[1]{0:T(128)} %bitcast.refs_0_, s32[1]{0:T(128)} %bitcast.1.refs_1_, s32[2,4]{1,0:T(2,128)S(1)} %copy-done.22, bf16[1536,384]{1,0:T(8,128)(2,1)S(1)} %copy-done.1, bf16[1536,384]{1,0:T(8,128)(2,1)S(1)} %copy-done.3, f32[8,384]{1,0:T(8,128)S(1)} %copy-done.15, ...), custom_call_target="tpu_custom_call" | custom-call | flops 5662310 | tf_op jit(solution)/shard_map/local/pallas_call | solution.py:82
  53.0 1.3 %back_step.5 = f32[8,384]{1,0:T(8,128)S(1)} custom-call(bf16[768,384]{1,0:T(8,128)(2,1)S(1)} %get-tuple-element.49.refs_0_.refs_1_, f32[8,384]{1,0:T(8,128)S(1)} %copy-done.11, bf16[768,384]{1,0:T(8,128)(2,1)S(1)} %get-tuple-element.64.refs_2_, f32[8,384]{1,0:T(8,128)S(1)} %copy-done.9, f32[8,384]{1,0:T(8,128)S(1)} %copy-done.13, ...), custom_call_target="tpu_custom_call" | custom-call | flops 2264924 | tf_op jit(solution)/shard_map/back_step/pallas_call | solution.py:82
  54.3 1.3 %collective-permute-start.14 = (f32[8,384]{1,0:T(8,128)S(1)}, f32[8,384]{1,0:T(8,128)S(1)}, u32[]{:S(2)}, u32[]{:S(2)}) collective-permute-start(f32[8,384]{1,0:T(8,128)S(1)} %back_step.5), channel_id=1, source_target_pairs={{448,384},{480,416},{320,256},{352,288},{192,128},{224,160},{64,0}... | collective-permute-start | bytes 36872 | tf_op jit(solution)/shard_map/ppermute | solution.py:427
  55.6 18.4 %collective-permute-done.14.refs_8_ = f32[8,384]{1,0:T(8,128)S(1)} collective-permute-done((f32[8,384]{1,0:T(8,128)S(1)}, f32[8,384]{1,0:T(8,128)S(1)}, u32[]{:S(2)}, u32[]{:S(2)}) %collective-permute-start.14) | collective-permute-done | bytes 12320 | tf_op jit(solution)/shard_map/ppermute | solution.py:427
  75.3 1.9 %collective-permute-start.15 = (f32[8,384]{1,0:T(8,128)S(1)}, f32[8,384]{1,0:T(8,128)S(1)}, u32[]{:S(2)}, u32[]{:S(2)}) collective-permute-start(f32[8,384]{1,0:T(8,128)S(1)} %get-tuple-element.73), channel_id=1, source_target_pairs={{0,32},{32,0},{64,96},{96,64},{128,160},{160,128},{192,224},{224,1... | collective-permute-start | bytes 36872 | tf_op jit(solution)/shard_map/ppermute | solution.py:433
  78.4 1.3 %last.1 = (f32[2,2,384]{2,1,0:T(2,128)}, f32[8,384]{1,0:T(8,128)S(1)}, f32[8,384]{1,0:T(8,128)S(1)}) custom-call(s32[1]{0:T(128)} %bitcast.refs_0_, f32[8,384]{1,0:T(8,128)S(1)} %collective-permute-done.15.refs_1_, f32[8,384]{1,0:T(8,128)S(1)} %get-tuple-element.74.refs_2_, f32[2,2,384]{2,1,0:T(2,128)S(1)} %get-tuple-element.72.refs_9_.refs_3_, ...), custom_call_target="tpu_custom_call" | custom-call | flops 5662310 | tf_op jit(solution)/shard_map/last/pallas_call | solution.py:82
  79.7 3.4 %collective-permute-start.16 = (f32[8,384]{1,0:T(8,128)S(1)}, f32[8,384]{1,0:T(8,128)S(1)}, u32[]{:S(2)}, u32[]{:S(2)}) collective-permute-start(f32[8,384]{1,0:T(8,128)S(1)} %get-tuple-element.79.refs_1_), channel_id=1, source_target_pairs={{0,1},{2,3},{4,5},{6,7},{8,9},{10,11},{12,13},{14,15},{16,17},{18,... | collective-permute-start | bytes 36872 | tf_op jit(solution)/shard_map/ppermute | solution.py:440
  83.1 15.5 %collective-permute-start.17 = (f32[8,384]{1,0:T(8,128)S(1)}, f32[8,384]{1,0:T(8,128)S(1)}, u32[]{:S(2)}, u32[]{:S(2)}) collective-permute-start(f32[8,384]{1,0:T(8,128)S(1)} %get-tuple-element.79.refs_1_), channel_id=1, source_target_pairs={{1,2},{3,4},{5,6},{7,8},{9,10},{11,12},{13,14},{15,16},{17,18},{19... | collective-permute-start | bytes 36872 | tf_op jit(solution)/shard_map/ppermute | solution.py:441
  98.6 3.0 %collective-permute-done.17.refs_3_ = f32[8,384]{1,0:T(8,128)S(1)} collective-permute-done((f32[8,384]{1,0:T(8,128)S(1)}, f32[8,384]{1,0:T(8,128)S(1)}, u32[]{:S(2)}, u32[]{:S(2)}) %collective-permute-start.17) | collective-permute-done | bytes 12320 | tf_op jit(solution)/shard_map/ppermute | solution.py:441
  (79 shorter events, 17.8 us)
Async XLA Ops:
  7.8 6.5 %collective-permute-start = (f32[1160,384]{1,0:T(8,128)}, f32[1160,384]{1,0:T(8,128)S(1)}, u32[]{:S(2)}, u32[]{:S(2)}) collective-permute-start(f32[1160,384]{1,0:T(8,128)} %get-tuple-element.41), channel_id=1, source_target_pairs={{0,32},{32,0},{64,96},{96,64},{128,160},{160,128},{192,224},{224,1... | collective-permute-start | bytes 5345288 | tf_op jit(solution)/shard_map/ppermute | solution.py:359
  15.3 18.7 %collective-permute-start.2 = (f32[392,384]{1,0:T(8,128)S(1)}, f32[392,384]{1,0:T(8,128)S(1)}, u32[]{:S(2)}, u32[]{:S(2)}) collective-permute-start(f32[392,384]{1,0:T(8,128)S(1)} %get-tuple-element.50), channel_id=1, source_target_pairs={{256,320},{288,352},{384,448},{416,480},{257,321},{289,353},{385,4... | collective-permute-start | bytes 1806344 | tf_op jit(solution)/shard_map/ppermute | solution.py:373
  17.4 16.7 %copy-start.4 = (bf16[768,384]{1,0:T(8,128)(2,1)}, bf16[768,384]{1,0:T(8,128)(2,1)S(1)}, u32[]{:S(2)}) copy-start(bf16[768,384]{1,0:T(8,128)(2,1)S(1)} %get-tuple-element.59.refs_3_) | copy-start | bytes 1769476
  17.4 18.6 %collective-permute-start.1 = (f32[384,384]{1,0:T(8,128)S(1)}, f32[384,384]{1,0:T(8,128)S(1)}, u32[]{:S(2)}, u32[]{:S(2)}) collective-permute-start(f32[384,384]{1,0:T(8,128)S(1)} %get-tuple-element.48), channel_id=1, source_target_pairs={{384,320},{416,352},{256,192},{288,224},{128,64},{160,96},{385,321... | collective-permute-start | bytes 1769480 | tf_op jit(solution)/shard_map/ppermute | solution.py:371
  19.5 0.7 collective-permute-start.3
  20.4 9.5 %collective-permute-start.4 = (f32[8,384]{1,0:T(8,128)S(1)}, f32[8,384]{1,0:T(8,128)S(1)}, u32[]{:S(2)}, u32[]{:S(2)}) collective-permute-start(f32[8,384]{1,0:T(8,128)S(1)} %step.3), channel_id=1, source_target_pairs={{64,128},{96,160},{65,129},{97,161},{66,130},{98,162},{67,131},{99... | collective-permute-start | bytes 36872 | tf_op jit(solution)/shard_map/ppermute | solution.py:379
  30.1 2.7 %collective-permute-start.5 = (f32[8,384]{1,0:T(8,128)S(1)}, f32[8,384]{1,0:T(8,128)S(1)}, u32[]{:S(2)}, u32[]{:S(2)}) collective-permute-start(f32[8,384]{1,0:T(8,128)S(1)} %step.4), channel_id=1, source_target_pairs={{128,192},{160,224},{129,193},{161,225},{130,194},{162,226},{131,1... | collective-permute-start | bytes 36872 | tf_op jit(solution)/shard_map/ppermute | solution.py:379
  33.1 1.0 collective-permute-start.6
  34.6 1.5 %collective-permute-start.7 = (f32[8,384]{1,0:T(8,128)S(1)}, f32[8,384]{1,0:T(8,128)S(1)}, u32[]{:S(2)}, u32[]{:S(2)}) collective-permute-start(f32[8,384]{1,0:T(8,128)S(1)} %jump_step.1), channel_id=1, source_target_pairs={{320,448},{352,480},{321,449},{353,481},{322,450},{354,482},{323,4... | collective-permute-start | bytes 36872 | tf_op jit(solution)/shard_map/ppermute | solution.py:384
  35.3 0.8 collective-permute-start.8
  37.2 7.2 %copy-start.10 = (f32[8,384]{1,0:T(8,128)}, f32[8,384]{1,0:T(8,128)S(1)}, u32[]{:S(2)}) copy-start(f32[8,384]{1,0:T(8,128)S(1)} %turn.1.refs_1_) | copy-start | bytes 36868
  37.2 2.7 %collective-permute-start.10 = (f32[8,384]{1,0:T(8,128)S(1)}, f32[8,384]{1,0:T(8,128)S(1)}, u32[]{:S(2)}, u32[]{:S(2)}) collective-permute-start(f32[8,384]{1,0:T(8,128)S(1)} %turn.1.refs_1_), channel_id=1, source_target_pairs={{384,320},{416,352},{256,192},{288,224},{128,64},{160,96},{385,321... | collective-permute-start | bytes 36872 | tf_op jit(solution)/shard_map/ppermute | solution.py:409
  38.5 1.4 %collective-permute-start.9 = (f32[8,384]{1,0:T(8,128)S(1)}, f32[8,384]{1,0:T(8,128)S(1)}, u32[]{:S(2)}, u32[]{:S(2)}) collective-permute-start(f32[8,384]{1,0:T(8,128)S(1)} %turn.1.refs_1_), channel_id=1, source_target_pairs={{448,320},{480,352},{449,321},{481,353},{450,322},{482,354},{451,3... | collective-permute-start | bytes 36872 | tf_op jit(solution)/shard_map/ppermute | solution.py:407
  40.4 3.9 %collective-permute-start.11 = (f32[8,384]{1,0:T(8,128)S(1)}, f32[8,384]{1,0:T(8,128)S(1)}, u32[]{:S(2)}, u32[]{:S(2)}) collective-permute-start(f32[8,384]{1,0:T(8,128)S(1)} %back_step.3), channel_id=1, source_target_pairs={{320,192},{352,224},{321,193},{353,225},{322,194},{354,226},{323,1... | collective-permute-start | bytes 36872 | tf_op jit(solution)/shard_map/ppermute | solution.py:407
  42.5 4.4 %collective-permute-start.13 = (f32[8,384]{1,0:T(8,128)}, f32[8,384]{1,0:T(8,128)}, u32[]{:S(2)}, u32[]{:S(2)}) collective-permute-start(f32[8,384]{1,0:T(8,128)} %get-tuple-element.69), channel_id=1, source_target_pairs={{0,32},{32,0},{64,96},{96,64},{128,160},{160,128},{192,224},{224,1... | collective-permute-start | bytes 36872 | tf_op jit(solution)/shard_map/ppermute | solution.py:416
  45.6 7.4 %collective-permute-start.12 = (f32[8,384]{1,0:T(8,128)}, f32[8,384]{1,0:T(8,128)}, u32[]{:S(2)}, u32[]{:S(2)}) collective-permute-start(f32[8,384]{1,0:T(8,128)} %back_step.4), channel_id=1, source_target_pairs={{192,64},{224,96},{193,65},{225,97},{194,66},{226,98},{195,67},{22... | collective-permute-start | bytes 36872 | tf_op jit(solution)/shard_map/ppermute | solution.py:407
  53.0 21.1 %copy-start.5 = (bf16[768,384]{1,0:T(8,128)(2,1)S(1)}, bf16[768,384]{1,0:T(8,128)(2,1)}, u32[]{:S(2)}) copy-start(bf16[768,384]{1,0:T(8,128)(2,1)} %copy-done.4) | copy-start | bytes 1769476
  53.0 21.1 %copy-start.19 = (f32[8,384]{1,0:T(8,128)S(1)}, f32[8,384]{1,0:T(8,128)}, u32[]{:S(2)}) copy-start(f32[8,384]{1,0:T(8,128)} %copy-done.18) | copy-start | bytes 36868
  53.0 25.3 %copy-start.6 = (bf16[384,384]{1,0:T(8,128)(2,1)S(1)}, bf16[384,384]{1,0:T(8,128)(2,1)}, u32[]{:S(2)}) copy-start(bf16[384,384]{1,0:T(8,128)(2,1)} %refs_6_.1) | copy-start | bytes 884740
  54.3 19.7 %collective-permute-start.14 = (f32[8,384]{1,0:T(8,128)S(1)}, f32[8,384]{1,0:T(8,128)S(1)}, u32[]{:S(2)}, u32[]{:S(2)}) collective-permute-start(f32[8,384]{1,0:T(8,128)S(1)} %back_step.5), channel_id=1, source_target_pairs={{448,384},{480,416},{320,256},{352,288},{192,128},{224,160},{64,0}... | collective-permute-start | bytes 36872 | tf_op jit(solution)/shard_map/ppermute | solution.py:427
  75.3 3.1 %collective-permute-start.15 = (f32[8,384]{1,0:T(8,128)S(1)}, f32[8,384]{1,0:T(8,128)S(1)}, u32[]{:S(2)}, u32[]{:S(2)}) collective-permute-start(f32[8,384]{1,0:T(8,128)S(1)} %get-tuple-element.73), channel_id=1, source_target_pairs={{0,32},{32,0},{64,96},{96,64},{128,160},{160,128},{192,224},{224,1... | collective-permute-start | bytes 36872 | tf_op jit(solution)/shard_map/ppermute | solution.py:433
  78.4 23.2 %copy-start.7 = (bf16[384,384]{1,0:T(8,128)(2,1)S(1)}, bf16[384,384]{1,0:T(8,128)(2,1)}, u32[]{:S(2)}) copy-start(bf16[384,384]{1,0:T(8,128)(2,1)} %refs_5_.1) | copy-start | bytes 884740
  79.7 18.9 %collective-permute-start.16 = (f32[8,384]{1,0:T(8,128)S(1)}, f32[8,384]{1,0:T(8,128)S(1)}, u32[]{:S(2)}, u32[]{:S(2)}) collective-permute-start(f32[8,384]{1,0:T(8,128)S(1)} %get-tuple-element.79.refs_1_), channel_id=1, source_target_pairs={{0,1},{2,3},{4,5},{6,7},{8,9},{10,11},{12,13},{14,15},{16,17},{18,... | collective-permute-start | bytes 36872 | tf_op jit(solution)/shard_map/ppermute | solution.py:440
  83.1 18.5 %collective-permute-start.17 = (f32[8,384]{1,0:T(8,128)S(1)}, f32[8,384]{1,0:T(8,128)S(1)}, u32[]{:S(2)}, u32[]{:S(2)}) collective-permute-start(f32[8,384]{1,0:T(8,128)S(1)} %get-tuple-element.79.refs_1_), channel_id=1, source_target_pairs={{1,2},{3,4},{5,6},{7,8},{9,10},{11,12},{13,14},{15,16},{17,18},{19... | collective-permute-start | bytes 36872 | tf_op jit(solution)/shard_map/ppermute | solution.py:441
  (18 other events, 41.0 us)

commit v3 on v2

--- a/solution.py
+++ b/solution.py
@@ -409,6 +409,7 @@
             sent = lax.ppermute(b_chip, "wall", chips_to([(j, j - 1) for j in range(chips - 2, 0, -2)]))
         if k == 1:
             done = out
+            upper_ends = lax.ppermute(out, "wall", chips_to([(j, j - 1) for j in odd[:-1]]))
             b_up, give, keep = call(
                 functools.partial(spread_kernel, jumps), [row] * 3, own_line, pre, a_low, lower, v_high, g_high, *y, *x,
                 scalars=1, flops=mul // 50, name="spread",
@@ -424,10 +425,10 @@
             functools.partial(jump_step_kernel, len(z)), [row], entry, b_chip, back, *z, sent,
             flops=mul // 50, name="back_step", after=waits,
         )
-    ends = lax.ppermute(out, "wall", chips_to([(k, k - 1) for k in odd]))
+    ends = lax.ppermute(out, "wall", chips_to([(1, 0)]))
 
     give, keep = call(
-        functools.partial(middle_kernel, len(z)), [row] * 2, own_line, entry, b_up, b_high, *z, sent, ends,
+        functools.partial(middle_kernel, len(z)), [row] * 2, own_line, entry, b_up, b_high, *z, sent, ends, upper_ends,
         scalars=1, flops=mul // 100, name="middle", after=(forward,),
     )
     got = lax.ppermute(give, "wall", across)

time: 103 us -> 102 us (level)
  waiting for transfers between devices: 32.9 us -> 31.1 us
    ppermute x1 -> x2, waiting for transfers between devices: 18.4 us -> 16.6 us  [the longest x1 16.6 us: body(): lax.ppermute(out, 'wall', chips_to([(j, j - 1) for j in odd[:-1]]))]
    ppermute x1 -> x2, starting transfers between devices: 1.31 us -> 2.11 us  [the longest x1 1.42 us: body(): lax.ppermute(out, 'wall', chips_to([(j, j - 1) for j in odd[:-1]]))]
  transfers between devices with their start and end apart: 18 -> 19, of which waited for: 6 -> 6; matrix products, arithmetic and copies ran while one was open for 0% -> 0% of each run, Pallas kernels for 10% -> 11%
where the time goes in v3:
time: 102 us; the launch traced here: 101 us
  starting transfers between devices  39 us (38%)
  waiting for transfers between devices  31.1 us (30%)
  Pallas kernels  23.6 us (23%)
  local copies, waits for them, and re-layouts  6.45 us (6%)
  between operations  1.34 us (1%)
    pallas_call x18, Pallas kernels, call(): pl.pallas_call(inner, out_shape=[jax.ShapeDtypeStruct(s, t) for s, t in o...  17.1 us
    ppermute x1, waiting for transfers between devices, body(): lax.ppermute(out, 'wall', chips_to([(j, j - 1) for j in odd[:-1]]))  16.6 us
    ppermute x1, starting transfers between devices, body(): from_far = lax.ppermute(sent, 'tang', second + [(j, i) for i, j in second])  15.5 us
    ppermute x3, waiting for transfers between devices, body(): x.append(lax.ppermute(out, 'wall', chips_to([(k - 1, k)])))  9.55 us
    pallas_call x1, Pallas kernels, body(): pl.pallas_call(first_kernel, out_shape=[jax.ShapeDtypeStruct(*x) for x in...  6.5 us
    unnamed x48, local copies, waits for them, and re-layouts  6.45 us
    ppermute x3, starting transfers between devices, body(): got = lax.ppermute(give, 'wall', across)  5.75 us
    ppermute x1, starting transfers between devices, body(): from_near = lax.ppermute(sent, 'tang', first + [(j, i) for i, j in first])  3.4 us
  transfers between devices with their start and end apart: 19, of which 6 were waited for; matrix products, arithmetic and copies ran while one was open for 0% of the time, Pallas kernels for 11%

profile of v3, /device:TPU:64, one launch (start us, length us, event | category | flops | bytes accessed | tf_op | source)
XLA Modules:
  0.0 101.4 jit_solution(14143567755437538009)
XLA Ops:
  1.3 6.5 %first.1 = (f32[1160,384]{1,0:T(8,128)}, bf16[1536,384]{1,0:T(8,128)(2,1)S(1)}, bf16[1536,384]{1,0:T(8,128)(2,1)S(1)}, f32[8,384]{1,0:T(8,128)S(1)}, f32[2,2,384...) custom-call(s32[1]{0:T(128)S(6)} %sub.3.line_ref, ...), custom_call_target="tpu_custom_call" | custom-call | flops 1472200704 | tf_op jit(solution)/shard_map/first/pallas_call | solution.py:349
  7.9 1.9 %collective-permute-start = (f32[1160,384]{1,0:T(8,128)}, f32[1160,384]{1,0:T(8,128)S(1)}, u32[]{:S(2)}, u32[]{:S(2)}) collective-permute-start(f32[1160,384]{1,0:T(8,128)} %get-tuple-element.41), channel_id=1, source_target_pairs={{0,32},{32,0},{64,96},{96,64},{128,160},{160,128},{192,224},{224,1... | collective-permute-start | bytes 5345288 | tf_op jit(solution)/shard_map/ppermute | solution.py:359
  9.8 3.5 %second.1 = (f32[1160,384]{1,0:T(8,128)S(1)}, bf16[1536,384]{1,0:T(8,128)(2,1)S(1)}, bf16[1536,384]{1,0:T(8,128)(2,1)S(1)}, f32[8,384]{1,0:T(8,128)S(1)}) custom-call(s32[1]{0:T(128)} %bitcast.refs_0_, f32[2,2,384]{2,1,0:T(2,128)S(1)} %get-tuple-element.42.refs_1_, bf16[2,2,384,384]{3,2,1,0:T(8,128)(2,1)S(1)} %get-tuple-element.43.refs_2_, ...), custom_call_target="tpu_custom_call" | custom-call | flops 1472200704 | tf_op jit(solution)/shard_map/second/pallas_call | solution.py:82
  16.0 1.4 %up_join.1 = (f32[384,384]{1,0:T(8,128)S(1)}, bf16[768,384]{1,0:T(8,128)(2,1)S(1)}, bf16[768,384]{1,0:T(8,128)(2,1)S(1)}, bf16[768,384]{1,0:T(8,128)(2,1)S(1)}, ...) custom-call(s32[1]{0:T(128)} %bitcast.refs_0_, ...), custom_call_target="tpu_custom_call" | custom-call | flops 339738624 | tf_op jit(solution)/shard_map/up_join/pallas_call | solution.py:82
  17.4 2.0 %collective-permute-start.1 = (f32[384,384]{1,0:T(8,128)S(1)}, f32[384,384]{1,0:T(8,128)S(1)}, u32[]{:S(2)}, u32[]{:S(2)}) collective-permute-start(f32[384,384]{1,0:T(8,128)S(1)} %get-tuple-element.48), channel_id=1, source_target_pairs={{384,320},{416,352},{256,192},{288,224},{128,64},{160,96},{385,321... | collective-permute-start | bytes 1769480 | tf_op jit(solution)/shard_map/ppermute | solution.py:371
  20.4 1.3 %collective-permute-start.4 = (f32[8,384]{1,0:T(8,128)S(1)}, f32[8,384]{1,0:T(8,128)S(1)}, u32[]{:S(2)}, u32[]{:S(2)}) collective-permute-start(f32[8,384]{1,0:T(8,128)S(1)} %step.3), channel_id=1, source_target_pairs={{64,128},{96,160},{65,129},{97,161},{66,130},{98,162},{67,131},{99... | collective-permute-start | bytes 36872 | tf_op jit(solution)/shard_map/ppermute | solution.py:379
  21.7 8.2 %collective-permute-done.4.refs_3_.refs_5_.refs_9_.refs_11_ = f32[8,384]{1,0:T(8,128)S(1)} collective-permute-done((f32[8,384]{1,0:T(8,128)S(1)}, f32[8,384]{1,0:T(8,128)S(1)}, u32[]{:S(2)}, u32[]{:S(2)}) %collective-permute-start.4) | collective-permute-done | bytes 12320 | tf_op jit(solution)/shard_map/ppermute | solution.py:379
  30.1 1.3 %collective-permute-start.5 = (f32[8,384]{1,0:T(8,128)S(1)}, f32[8,384]{1,0:T(8,128)S(1)}, u32[]{:S(2)}, u32[]{:S(2)}) collective-permute-start(f32[8,384]{1,0:T(8,128)S(1)} %step.4), channel_id=1, source_target_pairs={{128,192},{160,224},{129,193},{161,225},{130,194},{162,226},{131,1... | collective-permute-start | bytes 36872 | tf_op jit(solution)/shard_map/ppermute | solution.py:379
  31.5 1.4 %collective-permute-done.5.refs_4_.refs_6_.refs_10_.refs_12_ = f32[8,384]{1,0:T(8,128)S(1)} collective-permute-done((f32[8,384]{1,0:T(8,128)S(1)}, f32[8,384]{1,0:T(8,128)S(1)}, u32[]{:S(2)}, u32[]{:S(2)}) %collective-permute-start.5) | collective-permute-done | bytes 12320 | tf_op jit(solution)/shard_map/ppermute | solution.py:379
  37.2 1.3 %collective-permute-start.10 = (f32[8,384]{1,0:T(8,128)S(1)}, f32[8,384]{1,0:T(8,128)S(1)}, u32[]{:S(2)}, u32[]{:S(2)}) collective-permute-start(f32[8,384]{1,0:T(8,128)S(1)} %turn.1.refs_1_), channel_id=1, source_target_pairs={{384,320},{416,352},{256,192},{288,224},{128,64},{160,96},{385,321... | collective-permute-start | bytes 36872 | tf_op jit(solution)/shard_map/ppermute | solution.py:409
  41.2 1.2 %spread.1 = (f32[8,384]{1,0:T(8,128)S(1)}, f32[8,384]{1,0:T(8,128)}, f32[8,384]{1,0:T(8,128)S(1)}) custom-call(s32[1]{0:T(128)} %bitcast.refs_0_, bf16[768,384]{1,0:T(8,128)(2,1)S(1)} %get-tuple-element.51.refs_0_.refs_1_, f32[8,384]{1,0:T(8,128)S(1)} %get-tuple-element.52.refs_2_.refs_1_, bf16[768,384]{1,0:T(8,128)(2,1)S(1)} %get-tuple-element.53.refs_3_.refs_2_, ...), custom_call_target="tpu_custom_call" | custom-call | flops 2264924 | tf_op jit(solution)/shard_map/spread/pallas_call | solution.py:82
  42.5 1.9 %collective-permute-start.13 = (f32[8,384]{1,0:T(8,128)}, f32[8,384]{1,0:T(8,128)}, u32[]{:S(2)}, u32[]{:S(2)}) collective-permute-start(f32[8,384]{1,0:T(8,128)} %get-tuple-element.69), channel_id=1, source_target_pairs={{0,32},{32,0},{64,96},{96,64},{128,160},{160,128},{192,224},{224,1... | collective-permute-start | bytes 36872 | tf_op jit(solution)/shard_map/ppermute | solution.py:417
  45.6 1.3 %collective-permute-start.12 = (f32[8,384]{1,0:T(8,128)}, f32[8,384]{1,0:T(8,128)}, u32[]{:S(2)}, u32[]{:S(2)}) collective-permute-start(f32[8,384]{1,0:T(8,128)} %back_step.4), channel_id=1, source_target_pairs={{192,64},{224,96},{193,65},{225,97},{194,66},{226,98},{195,67},{22... | collective-permute-start | bytes 36872 | tf_op jit(solution)/shard_map/ppermute | solution.py:407
  46.8 1.3 %copy-done.1 = bf16[1536,384]{1,0:T(8,128)(2,1)S(1)} copy-done((bf16[1536,384]{1,0:T(8,128)(2,1)S(1)}, bf16[1536,384]{1,0:T(8,128)(2,1)}, u32[]{:S(2)}) %copy-start.1) | copy-done | bytes 1179672
  48.1 1.3 %copy-done.3 = bf16[1536,384]{1,0:T(8,128)(2,1)S(1)} copy-done((bf16[1536,384]{1,0:T(8,128)(2,1)S(1)}, bf16[1536,384]{1,0:T(8,128)(2,1)}, u32[]{:S(2)}) %copy-start.3) | copy-done | bytes 1179672
  51.5 1.5 %local.1 = (f32[2,2,384]{2,1,0:T(2,128)S(1)}, f32[2,8,384]{2,1,0:T(8,128)S(1)}) custom-call(s32[1]{0:T(128)} %bitcast.refs_0_, s32[1]{0:T(128)} %bitcast.1.refs_1_, s32[2,4]{1,0:T(2,128)S(1)} %copy-done.22, bf16[1536,384]{1,0:T(8,128)(2,1)S(1)} %copy-done.1, bf16[1536,384]{1,0:T(8,128)(2,1)S(1)} %copy-done.3, f32[8,384]{1,0:T(8,128)S(1)} %copy-done.15, ...), custom_call_target="tpu_custom_call" | custom-call | flops 5662310 | tf_op jit(solution)/shard_map/local/pallas_call | solution.py:82
  53.0 1.4 %collective-permute-start.15 = (f32[8,384]{1,0:T(8,128)}, f32[8,384]{1,0:T(8,128)S(1)}, u32[]{:S(2)}, u32[]{:S(2)}) collective-permute-start(f32[8,384]{1,0:T(8,128)} %back_step.4), channel_id=1, source_target_pairs={{448,384},{480,416},{320,256},{352,288},{192,128},{224,160},{449,3... | collective-permute-start | bytes 36872 | tf_op jit(solution)/shard_map/ppermute | solution.py:412
  54.5 1.2 %back_step.5 = f32[8,384]{1,0:T(8,128)S(1)} custom-call(bf16[768,384]{1,0:T(8,128)(2,1)S(1)} %get-tuple-element.49.refs_0_.refs_1_, f32[8,384]{1,0:T(8,128)S(1)} %copy-done.11, bf16[768,384]{1,0:T(8,128)(2,1)S(1)} %get-tuple-element.64.refs_2_, f32[8,384]{1,0:T(8,128)S(1)} %copy-done.9, f32[8,384]{1,0:T(8,128)S(1)} %copy-done.13, ...), custom_call_target="tpu_custom_call" | custom-call | flops 2264924 | tf_op jit(solution)/shard_map/back_step/pallas_call | solution.py:82
  56.4 16.6 %collective-permute-done.15.refs_9_ = f32[8,384]{1,0:T(8,128)S(1)} collective-permute-done((f32[8,384]{1,0:T(8,128)}, f32[8,384]{1,0:T(8,128)S(1)}, u32[]{:S(2)}, u32[]{:S(2)}) %collective-permute-start.15) | collective-permute-done | bytes 12320 | tf_op jit(solution)/shard_map/ppermute | solution.py:412
  74.3 1.9 %collective-permute-start.16 = (f32[8,384]{1,0:T(8,128)S(1)}, f32[8,384]{1,0:T(8,128)S(1)}, u32[]{:S(2)}, u32[]{:S(2)}) collective-permute-start(f32[8,384]{1,0:T(8,128)S(1)} %get-tuple-element.73), channel_id=1, source_target_pairs={{0,32},{32,0},{64,96},{96,64},{128,160},{160,128},{192,224},{224,1... | collective-permute-start | bytes 36872 | tf_op jit(solution)/shard_map/ppermute | solution.py:434
  77.4 1.3 %last.1 = (f32[2,2,384]{2,1,0:T(2,128)}, f32[8,384]{1,0:T(8,128)S(1)}, f32[8,384]{1,0:T(8,128)S(1)}) custom-call(s32[1]{0:T(128)} %bitcast.refs_0_, f32[8,384]{1,0:T(8,128)S(1)} %collective-permute-done.16.refs_1_, f32[8,384]{1,0:T(8,128)S(1)} %get-tuple-element.74.refs_2_, f32[2,2,384]{2,1,0:T(2,128)S(1)} %get-tuple-element.72.refs_10_.refs_3_, ...), custom_call_target="tpu_custom_call" | custom-call | flops 5662310 | tf_op jit(solution)/shard_map/last/pallas_call | solution.py:82
  78.7 3.4 %collective-permute-start.17 = (f32[8,384]{1,0:T(8,128)S(1)}, f32[8,384]{1,0:T(8,128)S(1)}, u32[]{:S(2)}, u32[]{:S(2)}) collective-permute-start(f32[8,384]{1,0:T(8,128)S(1)} %get-tuple-element.79.refs_1_), channel_id=1, source_target_pairs={{0,1},{2,3},{4,5},{6,7},{8,9},{10,11},{12,13},{14,15},{16,17},{18,... | collective-permute-start | bytes 36872 | tf_op jit(solution)/shard_map/ppermute | solution.py:441
  82.1 15.5 %collective-permute-start.18 = (f32[8,384]{1,0:T(8,128)S(1)}, f32[8,384]{1,0:T(8,128)S(1)}, u32[]{:S(2)}, u32[]{:S(2)}) collective-permute-start(f32[8,384]{1,0:T(8,128)S(1)} %get-tuple-element.79.refs_1_), channel_id=1, source_target_pairs={{1,2},{3,4},{5,6},{7,8},{9,10},{11,12},{13,14},{15,16},{17,18},{19... | collective-permute-start | bytes 36872 | tf_op jit(solution)/shard_map/ppermute | solution.py:442
  97.6 3.0 %collective-permute-done.18.refs_3_ = f32[8,384]{1,0:T(8,128)S(1)} collective-permute-done((f32[8,384]{1,0:T(8,128)S(1)}, f32[8,384]{1,0:T(8,128)S(1)}, u32[]{:S(2)}, u32[]{:S(2)}) %collective-permute-start.18) | collective-permute-done | bytes 12320 | tf_op jit(solution)/shard_map/ppermute | solution.py:442
  (81 shorter events, 18.5 us)
Async XLA Ops:
  7.9 6.5 %collective-permute-start = (f32[1160,384]{1,0:T(8,128)}, f32[1160,384]{1,0:T(8,128)S(1)}, u32[]{:S(2)}, u32[]{:S(2)}) collective-permute-start(f32[1160,384]{1,0:T(8,128)} %get-tuple-element.41), channel_id=1, source_target_pairs={{0,32},{32,0},{64,96},{96,64},{128,160},{160,128},{192,224},{224,1... | collective-permute-start | bytes 5345288 | tf_op jit(solution)/shard_map/ppermute | solution.py:359
  15.3 18.7 %collective-permute-start.2 = (f32[392,384]{1,0:T(8,128)S(1)}, f32[392,384]{1,0:T(8,128)S(1)}, u32[]{:S(2)}, u32[]{:S(2)}) collective-permute-start(f32[392,384]{1,0:T(8,128)S(1)} %get-tuple-element.50), channel_id=1, source_target_pairs={{256,320},{288,352},{384,448},{416,480},{257,321},{289,353},{385,4... | collective-permute-start | bytes 1806344 | tf_op jit(solution)/shard_map/ppermute | solution.py:373
  17.4 16.7 %copy-start.4 = (bf16[768,384]{1,0:T(8,128)(2,1)}, bf16[768,384]{1,0:T(8,128)(2,1)S(1)}, u32[]{:S(2)}) copy-start(bf16[768,384]{1,0:T(8,128)(2,1)S(1)} %get-tuple-element.59.refs_3_) | copy-start | bytes 1769476
  17.4 18.6 %collective-permute-start.1 = (f32[384,384]{1,0:T(8,128)S(1)}, f32[384,384]{1,0:T(8,128)S(1)}, u32[]{:S(2)}, u32[]{:S(2)}) collective-permute-start(f32[384,384]{1,0:T(8,128)S(1)} %get-tuple-element.48), channel_id=1, source_target_pairs={{384,320},{416,352},{256,192},{288,224},{128,64},{160,96},{385,321... | collective-permute-start | bytes 1769480 | tf_op jit(solution)/shard_map/ppermute | solution.py:371
  19.5 0.7 collective-permute-start.3
  20.4 9.5 %collective-permute-start.4 = (f32[8,384]{1,0:T(8,128)S(1)}, f32[8,384]{1,0:T(8,128)S(1)}, u32[]{:S(2)}, u32[]{:S(2)}) collective-permute-start(f32[8,384]{1,0:T(8,128)S(1)} %step.3), channel_id=1, source_target_pairs={{64,128},{96,160},{65,129},{97,161},{66,130},{98,162},{67,131},{99... | collective-permute-start | bytes 36872 | tf_op jit(solution)/shard_map/ppermute | solution.py:379
  30.1 2.7 %collective-permute-start.5 = (f32[8,384]{1,0:T(8,128)S(1)}, f32[8,384]{1,0:T(8,128)S(1)}, u32[]{:S(2)}, u32[]{:S(2)}) collective-permute-start(f32[8,384]{1,0:T(8,128)S(1)} %step.4), channel_id=1, source_target_pairs={{128,192},{160,224},{129,193},{161,225},{130,194},{162,226},{131,1... | collective-permute-start | bytes 36872 | tf_op jit(solution)/shard_map/ppermute | solution.py:379
  33.1 1.0 %collective-permute-start.6 = (f32[8,384]{1,0:T(8,128)S(1)}, f32[8,384]{1,0:T(8,128)S(1)}, u32[]{:S(2)}, u32[]{:S(2)}) collective-permute-start(f32[8,384]{1,0:T(8,128)S(1)} %step.5), channel_id=1, source_target_pairs={{192,320},{224,352},{193,321},{225,353},{194,322},{226,354},{195,3... | collective-permute-start | bytes 36872 | tf_op jit(solution)/shard_map/ppermute | solution.py:384
  34.6 1.5 %collective-permute-start.7 = (f32[8,384]{1,0:T(8,128)S(1)}, f32[8,384]{1,0:T(8,128)S(1)}, u32[]{:S(2)}, u32[]{:S(2)}) collective-permute-start(f32[8,384]{1,0:T(8,128)S(1)} %jump_step.1), channel_id=1, source_target_pairs={{320,448},{352,480},{321,449},{353,481},{322,450},{354,482},{323,4... | collective-permute-start | bytes 36872 | tf_op jit(solution)/shard_map/ppermute | solution.py:384
  35.3 0.8 collective-permute-start.8
  37.2 2.7 %collective-permute-start.10 = (f32[8,384]{1,0:T(8,128)S(1)}, f32[8,384]{1,0:T(8,128)S(1)}, u32[]{:S(2)}, u32[]{:S(2)}) collective-permute-start(f32[8,384]{1,0:T(8,128)S(1)} %turn.1.refs_1_), channel_id=1, source_target_pairs={{384,320},{416,352},{256,192},{288,224},{128,64},{160,96},{385,321... | collective-permute-start | bytes 36872 | tf_op jit(solution)/shard_map/ppermute | solution.py:409
  38.5 1.4 %collective-permute-start.9 = (f32[8,384]{1,0:T(8,128)S(1)}, f32[8,384]{1,0:T(8,128)S(1)}, u32[]{:S(2)}, u32[]{:S(2)}) collective-permute-start(f32[8,384]{1,0:T(8,128)S(1)} %turn.1.refs_1_), channel_id=1, source_target_pairs={{448,320},{480,352},{449,321},{481,353},{450,322},{482,354},{451,3... | collective-permute-start | bytes 36872 | tf_op jit(solution)/shard_map/ppermute | solution.py:407
  40.4 3.9 %collective-permute-start.11 = (f32[8,384]{1,0:T(8,128)S(1)}, f32[8,384]{1,0:T(8,128)S(1)}, u32[]{:S(2)}, u32[]{:S(2)}) collective-permute-start(f32[8,384]{1,0:T(8,128)S(1)} %back_step.3), channel_id=1, source_target_pairs={{320,192},{352,224},{321,193},{353,225},{322,194},{354,226},{323,1... | collective-permute-start | bytes 36872 | tf_op jit(solution)/shard_map/ppermute | solution.py:407
  42.5 4.3 %collective-permute-start.13 = (f32[8,384]{1,0:T(8,128)}, f32[8,384]{1,0:T(8,128)}, u32[]{:S(2)}, u32[]{:S(2)}) collective-permute-start(f32[8,384]{1,0:T(8,128)} %get-tuple-element.69), channel_id=1, source_target_pairs={{0,32},{32,0},{64,96},{96,64},{128,160},{160,128},{192,224},{224,1... | collective-permute-start | bytes 36872 | tf_op jit(solution)/shard_map/ppermute | solution.py:417
  45.6 8.9 %collective-permute-start.12 = (f32[8,384]{1,0:T(8,128)}, f32[8,384]{1,0:T(8,128)}, u32[]{:S(2)}, u32[]{:S(2)}) collective-permute-start(f32[8,384]{1,0:T(8,128)} %back_step.4), channel_id=1, source_target_pairs={{192,64},{224,96},{193,65},{225,97},{194,66},{226,98},{195,67},{22... | collective-permute-start | bytes 36872 | tf_op jit(solution)/shard_map/ppermute | solution.py:407
  52.9 20.1 %copy-start.5 = (bf16[768,384]{1,0:T(8,128)(2,1)S(1)}, bf16[768,384]{1,0:T(8,128)(2,1)}, u32[]{:S(2)}) copy-start(bf16[768,384]{1,0:T(8,128)(2,1)} %copy-done.4) | copy-start | bytes 1769476
  53.0 20.1 %copy-start.19 = (f32[8,384]{1,0:T(8,128)S(1)}, f32[8,384]{1,0:T(8,128)}, u32[]{:S(2)}) copy-start(f32[8,384]{1,0:T(8,128)} %copy-done.18) | copy-start | bytes 36868
  53.0 20.1 %collective-permute-start.15 = (f32[8,384]{1,0:T(8,128)}, f32[8,384]{1,0:T(8,128)S(1)}, u32[]{:S(2)}, u32[]{:S(2)}) collective-permute-start(f32[8,384]{1,0:T(8,128)} %back_step.4), channel_id=1, source_target_pairs={{448,384},{480,416},{320,256},{352,288},{192,128},{224,160},{449,3... | collective-permute-start | bytes 36872 | tf_op jit(solution)/shard_map/ppermute | solution.py:412
  54.5 22.9 %copy-start.6 = (bf16[384,384]{1,0:T(8,128)(2,1)S(1)}, bf16[384,384]{1,0:T(8,128)(2,1)}, u32[]{:S(2)}) copy-start(bf16[384,384]{1,0:T(8,128)(2,1)} %refs_6_.1) | copy-start | bytes 884740
  55.7 17.3 %collective-permute-start.14 = (f32[8,384]{1,0:T(8,128)S(1)}, f32[8,384]{1,0:T(8,128)S(1)}, u32[]{:S(2)}, u32[]{:S(2)}) collective-permute-start(f32[8,384]{1,0:T(8,128)S(1)} %back_step.5), channel_id=1, source_target_pairs={{64,0},{96,32},{65,1},{97,33},{66,2},{98,34},{67,3},{99,35},{68,4}... | collective-permute-start | bytes 36872 | tf_op jit(solution)/shard_map/ppermute | solution.py:428
  74.3 3.1 %collective-permute-start.16 = (f32[8,384]{1,0:T(8,128)S(1)}, f32[8,384]{1,0:T(8,128)S(1)}, u32[]{:S(2)}, u32[]{:S(2)}) collective-permute-start(f32[8,384]{1,0:T(8,128)S(1)} %get-tuple-element.73), channel_id=1, source_target_pairs={{0,32},{32,0},{64,96},{96,64},{128,160},{160,128},{192,224},{224,1... | collective-permute-start | bytes 36872 | tf_op jit(solution)/shard_map/ppermute | solution.py:434
  77.4 23.3 %copy-start.7 = (bf16[384,384]{1,0:T(8,128)(2,1)S(1)}, bf16[384,384]{1,0:T(8,128)(2,1)}, u32[]{:S(2)}) copy-start(bf16[384,384]{1,0:T(8,128)(2,1)} %refs_5_.1) | copy-start | bytes 884740
  78.7 18.9 %collective-permute-start.17 = (f32[8,384]{1,0:T(8,128)S(1)}, f32[8,384]{1,0:T(8,128)S(1)}, u32[]{:S(2)}, u32[]{:S(2)}) collective-permute-start(f32[8,384]{1,0:T(8,128)S(1)} %get-tuple-element.79.refs_1_), channel_id=1, source_target_pairs={{0,1},{2,3},{4,5},{6,7},{8,9},{10,11},{12,13},{14,15},{16,17},{18,... | collective-permute-start | bytes 36872 | tf_op jit(solution)/shard_map/ppermute | solution.py:441
  82.1 18.5 %collective-permute-start.18 = (f32[8,384]{1,0:T(8,128)S(1)}, f32[8,384]{1,0:T(8,128)S(1)}, u32[]{:S(2)}, u32[]{:S(2)}) collective-permute-start(f32[8,384]{1,0:T(8,128)S(1)} %get-tuple-element.79.refs_1_), channel_id=1, source_target_pairs={{1,2},{3,4},{5,6},{7,8},{9,10},{11,12},{13,14},{15,16},{17,18},{19... | collective-permute-start | bytes 36872 | tf_op jit(solution)/shard_map/ppermute | solution.py:442
  (19 other events, 52.5 us)

commit v4 on v3

--- a/solution.py
+++ b/solution.py
@@ -90,26 +90,29 @@
     )(*operands)
 
 
-def line_maps(a, l, u, r, out, ahead, back, rows):
+def line_maps(a, l, u, r, out, ahead, back, rows, sent=lambda part: None):
     n = r[0].shape[1]
     a0, l0 = a(0), l(0)
     first = dot(a0, l0)
     x = apply_exact(a0, r[0])
     a1, l1 = a(1), l(1)
     up = product(dot(a1, l1), first)
+    out[0:n] = up
+    sent(0)
     y = apply_exact(a1, r[1] - apply_exact(l1, x))
     u0 = u(0)
     near = dot(a0, u0)
     turn = -(first + product(near, up))
+    out[n : 2 * n] = turn
+    sent(1)
     x = x - apply_exact(a0, apply_exact(u0, y))
     far = dot(a1, u(1))
     down = product(near, far)
-    out[0:n] = up
-    out[n : 2 * n] = turn
     out[2 * n : 3 * n] = down
     index = lax.broadcasted_iota(jnp.int32, (8, n), 0)
     both = jnp.where(index == 0, jnp.broadcast_to(y, (8, n)), jnp.broadcast_to(x, (8, n)))
     out[3 * n :] = both
+    sent(2)
     rows[...] = both
     for ref, parts in ((ahead, (turn, up)), (back, (far, down))):
         for i, part in enumerate(parts):
@@ -118,7 +121,7 @@
             ref[(2 + i) * n : (3 + i) * n] = low
 
 
-def first_kernel(line_ref, r, a, l, u, out, ahead, back, rows, r_here, a_here, l_here, u_here, sems):
+def first_kernel(line_ref, r, a, l, u, given, ahead, back, rows, r_here, a_here, l_here, u_here, out, sems, out_sems):
     line = line_ref[0]
     copies = [pltpu.make_async_copy(r, r_here, sems.at[0])]
     for at in (line, 1 - line):
@@ -126,20 +129,29 @@
             (0, a, a_here), (0, l, l_here), (1, a, a_here), (1, l, l_here), (0, u, u_here), (1, u, u_here)
         ):
             copies.append(pltpu.make_async_copy(source.at[cell, at], here.at[cell, at], sems.at[len(copies)]))
-    for copy in copies:
+    for copy in copies[:7]:
         copy.start()
 
     def arrived(here, place):
         def get(cell):
             copies[place[cell]].wait()
+            if place[cell] == 5:
+                for copy in copies[7:]:
+                    copy.start()
             return here[cell, line]
 
         return get
+
+    n = r.shape[2]
+    parts = []
+    for i, (start, size) in enumerate(((0, n), (n, n), (2 * n, n + 8))):
+        at = pl.ds(start, size)
+        parts.append(pltpu.make_async_copy(out.at[at], given.at[at], out_sems.at[i]))
 
     copies[0].wait()
     blocks = [arrived(a_here, (1, 3)), arrived(l_here, (2, 4)), arrived(u_here, (5, 6))]
-    line_maps(*blocks, [r_here[cell, pl.ds(line, 1), :] for cell in range(2)], out, ahead, back, rows)
-    for copy in copies[7:]:
+    line_maps(*blocks, [r_here[cell, pl.ds(line, 1), :] for cell in range(2)], out, ahead, back, rows, lambda i: parts[i].start())
+    for copy in copies[7:] + parts:
         copy.wait()
 
 
@@ -350,8 +362,10 @@
         first_kernel,
         out_shape=[jax.ShapeDtypeStruct(*x) for x in maps + here_now],
         in_specs=[SMEM] + [HBM] * 4,
-        out_specs=[VMEM] * 8,
-        scratch_shapes=[pltpu.SemaphoreType.DMA((13,))],
+        out_specs=[HBM] + [VMEM] * 7,
+        scratch_shapes=[
+            pltpu.VMEM((3 * n + 8, n), F32), pltpu.SemaphoreType.DMA((13,)), pltpu.SemaphoreType.DMA((3,))
+        ],
         compiler_params=pltpu.CompilerParams(vmem_limit_bytes=WHOLE),
         cost_estimate=pl.CostEstimate(flops=13 * mul, bytes_accessed=0, transcendentals=0),
         name="first",

time: 102 us -> 102 us (level)
  no operation moved by 1% of the time
where the time goes in v4:
time: 102 us; the launch traced here: 101 us
  starting transfers between devices  39 us (38%)
  waiting for transfers between devices  31.1 us (30%)
  Pallas kernels  23.1 us (23%)
  local copies, waits for them, and re-layouts  6.45 us (6%)
  between operations  1.34 us (1%)
    pallas_call x18, Pallas kernels, call(): pl.pallas_call(inner, out_shape=[jax.ShapeDtypeStruct(s, t) for s, t in o...  17.1 us
    ppermute x1, waiting for transfers between devices, body(): lax.ppermute(out, 'wall', chips_to([(j, j - 1) for j in odd[:-1]]))  16.6 us
    ppermute x1, starting transfers between devices, body(): from_far = lax.ppermute(sent, 'tang', second + [(j, i) for i, j in second])  15.5 us
    ppermute x3, waiting for transfers between devices, body(): x.append(lax.ppermute(out, 'wall', chips_to([(k - 1, k)])))  9.55 us
    unnamed x48, local copies, waits for them, and re-layouts  6.45 us
    pallas_call x1, Pallas kernels, body(): pl.pallas_call(first_kernel, out_shape=[jax.ShapeDtypeStruct(*x) for x in...  5.99 us
    ppermute x3, starting transfers between devices, body(): got = lax.ppermute(give, 'wall', across)  5.75 us
    ppermute x1, starting transfers between devices, body(): from_near = lax.ppermute(sent, 'tang', first + [(j, i) for i, j in first])  3.4 us
  transfers between devices with their start and end apart: 19, of which 6 were waited for; matrix products, arithmetic and copies ran while one was open for 0% of the time, Pallas kernels for 11%

profile of v4, /device:TPU:64, one launch (start us, length us, event | category | flops | bytes accessed | tf_op | source)
XLA Modules:
  0.0 100.9 jit_solution(13801232123845220774)
XLA Ops:
  1.3 6.0 %first.1 = (f32[1160,384]{1,0:T(8,128)}, bf16[1536,384]{1,0:T(8,128)(2,1)S(1)}, bf16[1536,384]{1,0:T(8,128)(2,1)S(1)}, f32[8,384]{1,0:T(8,128)S(1)}, f32[2,2,384...) custom-call(s32[1]{0:T(128)S(6)} %sub.3.line_ref, ...), custom_call_target="tpu_custom_call" | custom-call | flops 1472200704 | tf_op jit(solution)/shard_map/first/pallas_call | solution.py:361
  7.3 1.9 %collective-permute-start = (f32[1160,384]{1,0:T(8,128)}, f32[1160,384]{1,0:T(8,128)S(1)}, u32[]{:S(2)}, u32[]{:S(2)}) collective-permute-start(f32[1160,384]{1,0:T(8,128)} %get-tuple-element.41), channel_id=1, source_target_pairs={{0,32},{32,0},{64,96},{96,64},{128,160},{160,128},{192,224},{224,1... | collective-permute-start | bytes 5345288 | tf_op jit(solution)/shard_map/ppermute | solution.py:373
  9.3 3.5 %second.1 = (f32[1160,384]{1,0:T(8,128)S(1)}, bf16[1536,384]{1,0:T(8,128)(2,1)S(1)}, bf16[1536,384]{1,0:T(8,128)(2,1)S(1)}, f32[8,384]{1,0:T(8,128)S(1)}) custom-call(s32[1]{0:T(128)} %bitcast.refs_0_, f32[2,2,384]{2,1,0:T(2,128)S(1)} %get-tuple-element.42.refs_1_, bf16[2,2,384,384]{3,2,1,0:T(8,128)(2,1)S(1)} %get-tuple-element.43.refs_2_, ...), custom_call_target="tpu_custom_call" | custom-call | flops 1472200704 | tf_op jit(solution)/shard_map/second/pallas_call | solution.py:82
  15.5 1.4 %up_join.1 = (f32[384,384]{1,0:T(8,128)S(1)}, bf16[768,384]{1,0:T(8,128)(2,1)S(1)}, bf16[768,384]{1,0:T(8,128)(2,1)S(1)}, bf16[768,384]{1,0:T(8,128)(2,1)S(1)}, ...) custom-call(s32[1]{0:T(128)} %bitcast.refs_0_, ...), custom_call_target="tpu_custom_call" | custom-call | flops 339738624 | tf_op jit(solution)/shard_map/up_join/pallas_call | solution.py:82
  16.9 2.0 %collective-permute-start.1 = (f32[384,384]{1,0:T(8,128)S(1)}, f32[384,384]{1,0:T(8,128)S(1)}, u32[]{:S(2)}, u32[]{:S(2)}) collective-permute-start(f32[384,384]{1,0:T(8,128)S(1)} %get-tuple-element.48), channel_id=1, source_target_pairs={{384,320},{416,352},{256,192},{288,224},{128,64},{160,96},{385,321... | collective-permute-start | bytes 1769480 | tf_op jit(solution)/shard_map/ppermute | solution.py:385
  19.9 1.3 %collective-permute-start.4 = (f32[8,384]{1,0:T(8,128)S(1)}, f32[8,384]{1,0:T(8,128)S(1)}, u32[]{:S(2)}, u32[]{:S(2)}) collective-permute-start(f32[8,384]{1,0:T(8,128)S(1)} %step.3), channel_id=1, source_target_pairs={{64,128},{96,160},{65,129},{97,161},{66,130},{98,162},{67,131},{99... | collective-permute-start | bytes 36872 | tf_op jit(solution)/shard_map/ppermute | solution.py:393
  21.2 8.2 %collective-permute-done.4.refs_3_.refs_5_.refs_9_.refs_11_ = f32[8,384]{1,0:T(8,128)S(1)} collective-permute-done((f32[8,384]{1,0:T(8,128)S(1)}, f32[8,384]{1,0:T(8,128)S(1)}, u32[]{:S(2)}, u32[]{:S(2)}) %collective-permute-start.4) | collective-permute-done | bytes 12320 | tf_op jit(solution)/shard_map/ppermute | solution.py:393
  29.6 1.3 %collective-permute-start.5 = (f32[8,384]{1,0:T(8,128)S(1)}, f32[8,384]{1,0:T(8,128)S(1)}, u32[]{:S(2)}, u32[]{:S(2)}) collective-permute-start(f32[8,384]{1,0:T(8,128)S(1)} %step.4), channel_id=1, source_target_pairs={{128,192},{160,224},{129,193},{161,225},{130,194},{162,226},{131,1... | collective-permute-start | bytes 36872 | tf_op jit(solution)/shard_map/ppermute | solution.py:393
  31.0 1.4 %collective-permute-done.5.refs_4_.refs_6_.refs_10_.refs_12_ = f32[8,384]{1,0:T(8,128)S(1)} collective-permute-done((f32[8,384]{1,0:T(8,128)S(1)}, f32[8,384]{1,0:T(8,128)S(1)}, u32[]{:S(2)}, u32[]{:S(2)}) %collective-permute-start.5) | collective-permute-done | bytes 12320 | tf_op jit(solution)/shard_map/ppermute | solution.py:393
  36.7 1.3 %collective-permute-start.10 = (f32[8,384]{1,0:T(8,128)S(1)}, f32[8,384]{1,0:T(8,128)S(1)}, u32[]{:S(2)}, u32[]{:S(2)}) collective-permute-start(f32[8,384]{1,0:T(8,128)S(1)} %turn.1.refs_1_), channel_id=1, source_target_pairs={{384,320},{416,352},{256,192},{288,224},{128,64},{160,96},{385,321... | collective-permute-start | bytes 36872 | tf_op jit(solution)/shard_map/ppermute | solution.py:423
  40.7 1.2 %spread.1 = (f32[8,384]{1,0:T(8,128)S(1)}, f32[8,384]{1,0:T(8,128)}, f32[8,384]{1,0:T(8,128)S(1)}) custom-call(s32[1]{0:T(128)} %bitcast.refs_0_, bf16[768,384]{1,0:T(8,128)(2,1)S(1)} %get-tuple-element.51.refs_0_.refs_1_, f32[8,384]{1,0:T(8,128)S(1)} %get-tuple-element.52.refs_2_.refs_1_, bf16[768,384]{1,0:T(8,128)(2,1)S(1)} %get-tuple-element.53.refs_3_.refs_2_, ...), custom_call_target="tpu_custom_call" | custom-call | flops 2264924 | tf_op jit(solution)/shard_map/spread/pallas_call | solution.py:82
  42.0 1.9 %collective-permute-start.13 = (f32[8,384]{1,0:T(8,128)}, f32[8,384]{1,0:T(8,128)}, u32[]{:S(2)}, u32[]{:S(2)}) collective-permute-start(f32[8,384]{1,0:T(8,128)} %get-tuple-element.69), channel_id=1, source_target_pairs={{0,32},{32,0},{64,96},{96,64},{128,160},{160,128},{192,224},{224,1... | collective-permute-start | bytes 36872 | tf_op jit(solution)/shard_map/ppermute | solution.py:431
  45.1 1.3 %collective-permute-start.12 = (f32[8,384]{1,0:T(8,128)}, f32[8,384]{1,0:T(8,128)}, u32[]{:S(2)}, u32[]{:S(2)}) collective-permute-start(f32[8,384]{1,0:T(8,128)} %back_step.4), channel_id=1, source_target_pairs={{192,64},{224,96},{193,65},{225,97},{194,66},{226,98},{195,67},{22... | collective-permute-start | bytes 36872 | tf_op jit(solution)/shard_map/ppermute | solution.py:421
  46.3 1.3 %copy-done.1 = bf16[1536,384]{1,0:T(8,128)(2,1)S(1)} copy-done((bf16[1536,384]{1,0:T(8,128)(2,1)S(1)}, bf16[1536,384]{1,0:T(8,128)(2,1)}, u32[]{:S(2)}) %copy-start.1) | copy-done | bytes 1179672
  47.6 1.3 %copy-done.3 = bf16[1536,384]{1,0:T(8,128)(2,1)S(1)} copy-done((bf16[1536,384]{1,0:T(8,128)(2,1)S(1)}, bf16[1536,384]{1,0:T(8,128)(2,1)}, u32[]{:S(2)}) %copy-start.3) | copy-done | bytes 1179672
  51.0 1.5 %local.1 = (f32[2,2,384]{2,1,0:T(2,128)S(1)}, f32[2,8,384]{2,1,0:T(8,128)S(1)}) custom-call(s32[1]{0:T(128)} %bitcast.refs_0_, s32[1]{0:T(128)} %bitcast.1.refs_1_, s32[2,4]{1,0:T(2,128)S(1)} %copy-done.22, bf16[1536,384]{1,0:T(8,128)(2,1)S(1)} %copy-done.1, bf16[1536,384]{1,0:T(8,128)(2,1)S(1)} %copy-done.3, f32[8,384]{1,0:T(8,128)S(1)} %copy-done.15, ...), custom_call_target="tpu_custom_call" | custom-call | flops 5662310 | tf_op jit(solution)/shard_map/local/pallas_call | solution.py:82
  52.5 1.4 %collective-permute-start.15 = (f32[8,384]{1,0:T(8,128)}, f32[8,384]{1,0:T(8,128)S(1)}, u32[]{:S(2)}, u32[]{:S(2)}) collective-permute-start(f32[8,384]{1,0:T(8,128)} %back_step.4), channel_id=1, source_target_pairs={{448,384},{480,416},{320,256},{352,288},{192,128},{224,160},{449,3... | collective-permute-start | bytes 36872 | tf_op jit(solution)/shard_map/ppermute | solution.py:426
  54.0 1.2 %back_step.5 = f32[8,384]{1,0:T(8,128)S(1)} custom-call(bf16[768,384]{1,0:T(8,128)(2,1)S(1)} %get-tuple-element.49.refs_0_.refs_1_, f32[8,384]{1,0:T(8,128)S(1)} %copy-done.11, bf16[768,384]{1,0:T(8,128)(2,1)S(1)} %get-tuple-element.64.refs_2_, f32[8,384]{1,0:T(8,128)S(1)} %copy-done.9, f32[8,384]{1,0:T(8,128)S(1)} %copy-done.13, ...), custom_call_target="tpu_custom_call" | custom-call | flops 2264924 | tf_op jit(solution)/shard_map/back_step/pallas_call | solution.py:82
  55.9 16.6 %collective-permute-done.15.refs_9_ = f32[8,384]{1,0:T(8,128)S(1)} collective-permute-done((f32[8,384]{1,0:T(8,128)}, f32[8,384]{1,0:T(8,128)S(1)}, u32[]{:S(2)}, u32[]{:S(2)}) %collective-permute-start.15) | collective-permute-done | bytes 12320 | tf_op jit(solution)/shard_map/ppermute | solution.py:426
  73.8 1.9 %collective-permute-start.16 = (f32[8,384]{1,0:T(8,128)S(1)}, f32[8,384]{1,0:T(8,128)S(1)}, u32[]{:S(2)}, u32[]{:S(2)}) collective-permute-start(f32[8,384]{1,0:T(8,128)S(1)} %get-tuple-element.73), channel_id=1, source_target_pairs={{0,32},{32,0},{64,96},{96,64},{128,160},{160,128},{192,224},{224,1... | collective-permute-start | bytes 36872 | tf_op jit(solution)/shard_map/ppermute | solution.py:448
  76.9 1.3 %last.1 = (f32[2,2,384]{2,1,0:T(2,128)}, f32[8,384]{1,0:T(8,128)S(1)}, f32[8,384]{1,0:T(8,128)S(1)}) custom-call(s32[1]{0:T(128)} %bitcast.refs_0_, f32[8,384]{1,0:T(8,128)S(1)} %collective-permute-done.16.refs_1_, f32[8,384]{1,0:T(8,128)S(1)} %get-tuple-element.74.refs_2_, f32[2,2,384]{2,1,0:T(2,128)S(1)} %get-tuple-element.72.refs_10_.refs_3_, ...), custom_call_target="tpu_custom_call" | custom-call | flops 5662310 | tf_op jit(solution)/shard_map/last/pallas_call | solution.py:82
  78.2 3.4 %collective-permute-start.17 = (f32[8,384]{1,0:T(8,128)S(1)}, f32[8,384]{1,0:T(8,128)S(1)}, u32[]{:S(2)}, u32[]{:S(2)}) collective-permute-start(f32[8,384]{1,0:T(8,128)S(1)} %get-tuple-element.79.refs_1_), channel_id=1, source_target_pairs={{0,1},{2,3},{4,5},{6,7},{8,9},{10,11},{12,13},{14,15},{16,17},{18,... | collective-permute-start | bytes 36872 | tf_op jit(solution)/shard_map/ppermute | solution.py:455
  81.6 15.5 %collective-permute-start.18 = (f32[8,384]{1,0:T(8,128)S(1)}, f32[8,384]{1,0:T(8,128)S(1)}, u32[]{:S(2)}, u32[]{:S(2)}) collective-permute-start(f32[8,384]{1,0:T(8,128)S(1)} %get-tuple-element.79.refs_1_), channel_id=1, source_target_pairs={{1,2},{3,4},{5,6},{7,8},{9,10},{11,12},{13,14},{15,16},{17,18},{19... | collective-permute-start | bytes 36872 | tf_op jit(solution)/shard_map/ppermute | solution.py:456
  97.1 3.0 %collective-permute-done.18.refs_3_ = f32[8,384]{1,0:T(8,128)S(1)} collective-permute-done((f32[8,384]{1,0:T(8,128)S(1)}, f32[8,384]{1,0:T(8,128)S(1)}, u32[]{:S(2)}, u32[]{:S(2)}) %collective-permute-start.18) | collective-permute-done | bytes 12320 | tf_op jit(solution)/shard_map/ppermute | solution.py:456
  (81 shorter events, 18.5 us)
Async XLA Ops:
  7.3 6.5 %collective-permute-start = (f32[1160,384]{1,0:T(8,128)}, f32[1160,384]{1,0:T(8,128)S(1)}, u32[]{:S(2)}, u32[]{:S(2)}) collective-permute-start(f32[1160,384]{1,0:T(8,128)} %get-tuple-element.41), channel_id=1, source_target_pairs={{0,32},{32,0},{64,96},{96,64},{128,160},{160,128},{192,224},{224,1... | collective-permute-start | bytes 5345288 | tf_op jit(solution)/shard_map/ppermute | solution.py:373
  14.8 18.7 %collective-permute-start.2 = (f32[392,384]{1,0:T(8,128)S(1)}, f32[392,384]{1,0:T(8,128)S(1)}, u32[]{:S(2)}, u32[]{:S(2)}) collective-permute-start(f32[392,384]{1,0:T(8,128)S(1)} %get-tuple-element.50), channel_id=1, source_target_pairs={{256,320},{288,352},{384,448},{416,480},{257,321},{289,353},{385,4... | collective-permute-start | bytes 1806344 | tf_op jit(solution)/shard_map/ppermute | solution.py:387
  16.9 16.7 %copy-start.4 = (bf16[768,384]{1,0:T(8,128)(2,1)}, bf16[768,384]{1,0:T(8,128)(2,1)S(1)}, u32[]{:S(2)}) copy-start(bf16[768,384]{1,0:T(8,128)(2,1)S(1)} %get-tuple-element.59.refs_3_) | copy-start | bytes 1769476
  16.9 18.6 %collective-permute-start.1 = (f32[384,384]{1,0:T(8,128)S(1)}, f32[384,384]{1,0:T(8,128)S(1)}, u32[]{:S(2)}, u32[]{:S(2)}) collective-permute-start(f32[384,384]{1,0:T(8,128)S(1)} %get-tuple-element.48), channel_id=1, source_target_pairs={{384,320},{416,352},{256,192},{288,224},{128,64},{160,96},{385,321... | collective-permute-start | bytes 1769480 | tf_op jit(solution)/shard_map/ppermute | solution.py:385
  19.0 0.7 collective-permute-start.3
  19.9 9.5 %collective-permute-start.4 = (f32[8,384]{1,0:T(8,128)S(1)}, f32[8,384]{1,0:T(8,128)S(1)}, u32[]{:S(2)}, u32[]{:S(2)}) collective-permute-start(f32[8,384]{1,0:T(8,128)S(1)} %step.3), channel_id=1, source_target_pairs={{64,128},{96,160},{65,129},{97,161},{66,130},{98,162},{67,131},{99... | collective-permute-start | bytes 36872 | tf_op jit(solution)/shard_map/ppermute | solution.py:393
  29.6 2.7 %collective-permute-start.5 = (f32[8,384]{1,0:T(8,128)S(1)}, f32[8,384]{1,0:T(8,128)S(1)}, u32[]{:S(2)}, u32[]{:S(2)}) collective-permute-start(f32[8,384]{1,0:T(8,128)S(1)} %step.4), channel_id=1, source_target_pairs={{128,192},{160,224},{129,193},{161,225},{130,194},{162,226},{131,1... | collective-permute-start | bytes 36872 | tf_op jit(solution)/shard_map/ppermute | solution.py:393
  32.6 1.0 %collective-permute-start.6 = (f32[8,384]{1,0:T(8,128)S(1)}, f32[8,384]{1,0:T(8,128)S(1)}, u32[]{:S(2)}, u32[]{:S(2)}) collective-permute-start(f32[8,384]{1,0:T(8,128)S(1)} %step.5), channel_id=1, source_target_pairs={{192,320},{224,352},{193,321},{225,353},{194,322},{226,354},{195,3... | collective-permute-start | bytes 36872 | tf_op jit(solution)/shard_map/ppermute | solution.py:398
  34.1 1.5 %collective-permute-start.7 = (f32[8,384]{1,0:T(8,128)S(1)}, f32[8,384]{1,0:T(8,128)S(1)}, u32[]{:S(2)}, u32[]{:S(2)}) collective-permute-start(f32[8,384]{1,0:T(8,128)S(1)} %jump_step.1), channel_id=1, source_target_pairs={{320,448},{352,480},{321,449},{353,481},{322,450},{354,482},{323,4... | collective-permute-start | bytes 36872 | tf_op jit(solution)/shard_map/ppermute | solution.py:398
  34.8 0.8 collective-permute-start.8
  36.7 2.7 %collective-permute-start.10 = (f32[8,384]{1,0:T(8,128)S(1)}, f32[8,384]{1,0:T(8,128)S(1)}, u32[]{:S(2)}, u32[]{:S(2)}) collective-permute-start(f32[8,384]{1,0:T(8,128)S(1)} %turn.1.refs_1_), channel_id=1, source_target_pairs={{384,320},{416,352},{256,192},{288,224},{128,64},{160,96},{385,321... | collective-permute-start | bytes 36872 | tf_op jit(solution)/shard_map/ppermute | solution.py:423
  38.0 1.4 %collective-permute-start.9 = (f32[8,384]{1,0:T(8,128)S(1)}, f32[8,384]{1,0:T(8,128)S(1)}, u32[]{:S(2)}, u32[]{:S(2)}) collective-permute-start(f32[8,384]{1,0:T(8,128)S(1)} %turn.1.refs_1_), channel_id=1, source_target_pairs={{448,320},{480,352},{449,321},{481,353},{450,322},{482,354},{451,3... | collective-permute-start | bytes 36872 | tf_op jit(solution)/shard_map/ppermute | solution.py:421
  39.9 3.9 %collective-permute-start.11 = (f32[8,384]{1,0:T(8,128)S(1)}, f32[8,384]{1,0:T(8,128)S(1)}, u32[]{:S(2)}, u32[]{:S(2)}) collective-permute-start(f32[8,384]{1,0:T(8,128)S(1)} %back_step.3), channel_id=1, source_target_pairs={{320,192},{352,224},{321,193},{353,225},{322,194},{354,226},{323,1... | collective-permute-start | bytes 36872 | tf_op jit(solution)/shard_map/ppermute | solution.py:421
  42.0 4.3 %collective-permute-start.13 = (f32[8,384]{1,0:T(8,128)}, f32[8,384]{1,0:T(8,128)}, u32[]{:S(2)}, u32[]{:S(2)}) collective-permute-start(f32[8,384]{1,0:T(8,128)} %get-tuple-element.69), channel_id=1, source_target_pairs={{0,32},{32,0},{64,96},{96,64},{128,160},{160,128},{192,224},{224,1... | collective-permute-start | bytes 36872 | tf_op jit(solution)/shard_map/ppermute | solution.py:431
  45.1 8.9 %collective-permute-start.12 = (f32[8,384]{1,0:T(8,128)}, f32[8,384]{1,0:T(8,128)}, u32[]{:S(2)}, u32[]{:S(2)}) collective-permute-start(f32[8,384]{1,0:T(8,128)} %back_step.4), channel_id=1, source_target_pairs={{192,64},{224,96},{193,65},{225,97},{194,66},{226,98},{195,67},{22... | collective-permute-start | bytes 36872 | tf_op jit(solution)/shard_map/ppermute | solution.py:421
  52.4 20.1 %copy-start.5 = (bf16[768,384]{1,0:T(8,128)(2,1)S(1)}, bf16[768,384]{1,0:T(8,128)(2,1)}, u32[]{:S(2)}) copy-start(bf16[768,384]{1,0:T(8,128)(2,1)} %copy-done.4) | copy-start | bytes 1769476
  52.5 20.1 %copy-start.19 = (f32[8,384]{1,0:T(8,128)S(1)}, f32[8,384]{1,0:T(8,128)}, u32[]{:S(2)}) copy-start(f32[8,384]{1,0:T(8,128)} %copy-done.18) | copy-start | bytes 36868
  52.5 20.1 %collective-permute-start.15 = (f32[8,384]{1,0:T(8,128)}, f32[8,384]{1,0:T(8,128)S(1)}, u32[]{:S(2)}, u32[]{:S(2)}) collective-permute-start(f32[8,384]{1,0:T(8,128)} %back_step.4), channel_id=1, source_target_pairs={{448,384},{480,416},{320,256},{352,288},{192,128},{224,160},{449,3... | collective-permute-start | bytes 36872 | tf_op jit(solution)/shard_map/ppermute | solution.py:426
  54.0 22.9 %copy-start.6 = (bf16[384,384]{1,0:T(8,128)(2,1)S(1)}, bf16[384,384]{1,0:T(8,128)(2,1)}, u32[]{:S(2)}) copy-start(bf16[384,384]{1,0:T(8,128)(2,1)} %refs_6_.1) | copy-start | bytes 884740
  55.2 17.3 %collective-permute-start.14 = (f32[8,384]{1,0:T(8,128)S(1)}, f32[8,384]{1,0:T(8,128)S(1)}, u32[]{:S(2)}, u32[]{:S(2)}) collective-permute-start(f32[8,384]{1,0:T(8,128)S(1)} %back_step.5), channel_id=1, source_target_pairs={{64,0},{96,32},{65,1},{97,33},{66,2},{98,34},{67,3},{99,35},{68,4}... | collective-permute-start | bytes 36872 | tf_op jit(solution)/shard_map/ppermute | solution.py:442
  73.8 3.1 %collective-permute-start.16 = (f32[8,384]{1,0:T(8,128)S(1)}, f32[8,384]{1,0:T(8,128)S(1)}, u32[]{:S(2)}, u32[]{:S(2)}) collective-permute-start(f32[8,384]{1,0:T(8,128)S(1)} %get-tuple-element.73), channel_id=1, source_target_pairs={{0,32},{32,0},{64,96},{96,64},{128,160},{160,128},{192,224},{224,1... | collective-permute-start | bytes 36872 | tf_op jit(solution)/shard_map/ppermute | solution.py:448
  76.9 23.3 %copy-start.7 = (bf16[384,384]{1,0:T(8,128)(2,1)S(1)}, bf16[384,384]{1,0:T(8,128)(2,1)}, u32[]{:S(2)}) copy-start(bf16[384,384]{1,0:T(8,128)(2,1)} %refs_5_.1) | copy-start | bytes 884740
  78.2 18.9 %collective-permute-start.17 = (f32[8,384]{1,0:T(8,128)S(1)}, f32[8,384]{1,0:T(8,128)S(1)}, u32[]{:S(2)}, u32[]{:S(2)}) collective-permute-start(f32[8,384]{1,0:T(8,128)S(1)} %get-tuple-element.79.refs_1_), channel_id=1, source_target_pairs={{0,1},{2,3},{4,5},{6,7},{8,9},{10,11},{12,13},{14,15},{16,17},{18,... | collective-permute-start | bytes 36872 | tf_op jit(solution)/shard_map/ppermute | solution.py:455
  81.6 18.5 %collective-permute-start.18 = (f32[8,384]{1,0:T(8,128)S(1)}, f32[8,384]{1,0:T(8,128)S(1)}, u32[]{:S(2)}, u32[]{:S(2)}) collective-permute-start(f32[8,384]{1,0:T(8,128)S(1)} %get-tuple-element.79.refs_1_), channel_id=1, source_target_pairs={{1,2},{3,4},{5,6},{7,8},{9,10},{11,12},{13,14},{15,16},{17,18},{19... | collective-permute-start | bytes 36872 | tf_op jit(solution)/shard_map/ppermute | solution.py:456
  (19 other events, 52.5 us)

commit v5 on v4

--- a/solution.py
+++ b/solution.py
@@ -235,8 +235,10 @@
 
 
 def jump_step_kernel(many, before, constant, pair, *refs):
-    *x, out = refs
-    put_row(out, constant[0:1] + apply_pair(pair[...], entering(before, x[:many], x[many:])))
+    *x, out, come = refs
+    enter = entering(before, x[:many], x[many:])
+    put_row(out, constant[0:1] + apply_pair(pair[...], enter))
+    put_row(come, enter)
 
 
 def turn_kernel(many, before, a_low, lower, v_low, v_high, b_low, g_low, g_high, *refs):
@@ -280,9 +282,9 @@
             weights[line, k : k + 1] = row
 
 
-def middle_kernel(many, core, before, b_up, b_high, *refs):
+def middle_kernel(core, b_up, b_high, *refs):
     *x, give, keep = refs
-    enter = entering(before, x[:many], x[many:])
+    enter = total_of(x)
     middle = b_up[0:1] + apply_pair(b_high[...], enter)
     first = core[0] == 0
     put_row(give, jnp.where(first, enter, middle))
@@ -401,8 +403,8 @@
                 out, "wall", chips_to([(singles + 2 * j - 1, singles + 2 * j) for j in range(jumps)])
             )
         else:
-            (out,) = call(
-                functools.partial(jump_step_kernel, k + 1), [row], pre, a_chip, total, *y, *x, pre_row,
+            out, _ = call(
+                functools.partial(jump_step_kernel, k + 1), [row] * 2, pre, a_chip, total, *y, *x, pre_row,
                 flops=mul // 50, name="jump_step",
             )
     x = [*x, side, pre_row]
@@ -435,14 +437,14 @@
                 scalars=3, flops=mul // 20, name="local",
             )
             waits = (weights,)
-        (out,) = call(
-            functools.partial(jump_step_kernel, len(z)), [row], entry, b_chip, back, *z, sent,
+        out, come = call(
+            functools.partial(jump_step_kernel, len(z)), [row] * 2, entry, b_chip, back, *z, sent,
             flops=mul // 50, name="back_step", after=waits,
         )
     ends = lax.ppermute(out, "wall", chips_to([(1, 0)]))
 
     give, keep = call(
-        functools.partial(middle_kernel, len(z)), [row] * 2, own_line, entry, b_up, b_high, *z, sent, ends, upper_ends,
+        middle_kernel, [row] * 2, own_line, b_up, b_high, come, ends, upper_ends,
         scalars=1, flops=mul // 100, name="middle", after=(forward,),
     )
     got = lax.ppermute(give, "wall", across)

time: 102 us -> 102 us (level)
  transfers between devices with their start and end apart: 19 -> 19, of which waited for: 6 -> 6; matrix products, arithmetic and copies ran while one was open for 0% -> 0% of each run, Pallas kernels for 11% -> 12%
where the time goes in v5:
time: 102 us; the launch traced here: 101 us
  starting transfers between devices  39 us (38%)
  waiting for transfers between devices  31.1 us (30%)
  Pallas kernels  23.1 us (23%)
  local copies, waits for them, and re-layouts  7.05 us (7%)
  between operations  1.2 us (1%)
    pallas_call x18, Pallas kernels, call(): pl.pallas_call(inner, out_shape=[jax.ShapeDtypeStruct(s, t) for s, t in o...  17.1 us
    ppermute x1, waiting for transfers between devices, body(): lax.ppermute(out, 'wall', chips_to([(j, j - 1) for j in odd[:-1]]))  16.7 us
    ppermute x1, starting transfers between devices, body(): from_far = lax.ppermute(sent, 'tang', second + [(j, i) for i, j in second])  15.5 us
    ppermute x3, waiting for transfers between devices, body(): x.append(lax.ppermute(out, 'wall', chips_to([(k - 1, k)])))  9.55 us
    unnamed x48, local copies, waits for them, and re-layouts  7.05 us
    pallas_call x1, Pallas kernels, body(): pl.pallas_call(first_kernel, out_shape=[jax.ShapeDtypeStruct(*x) for x in...  5.98 us
    ppermute x3, starting transfers between devices, body(): got = lax.ppermute(give, 'wall', across)  5.77 us
    ppermute x1, starting transfers between devices, body(): from_near = lax.ppermute(sent, 'tang', first + [(j, i) for i, j in first])  3.4 us
  transfers between devices with their start and end apart: 19, of which 6 were waited for; matrix products, arithmetic and copies ran while one was open for 0% of the time, Pallas kernels for 12%

profile of v5, /device:TPU:64, one launch (start us, length us, event | category | flops | bytes accessed | tf_op | source)
XLA Modules:
  0.0 101.5 jit_solution(17565749354375961996)
XLA Ops:
  1.3 6.0 %first.1 = (f32[1160,384]{1,0:T(8,128)}, bf16[1536,384]{1,0:T(8,128)(2,1)S(1)}, bf16[1536,384]{1,0:T(8,128)(2,1)S(1)}, f32[8,384]{1,0:T(8,128)S(1)}, f32[2,2,384...) custom-call(s32[1]{0:T(128)S(6)} %sub.3.line_ref, ...), custom_call_target="tpu_custom_call" | custom-call | flops 1472200704 | tf_op jit(solution)/shard_map/first/pallas_call | solution.py:363
  7.3 1.9 %collective-permute-start = (f32[1160,384]{1,0:T(8,128)}, f32[1160,384]{1,0:T(8,128)S(1)}, u32[]{:S(2)}, u32[]{:S(2)}) collective-permute-start(f32[1160,384]{1,0:T(8,128)} %get-tuple-element.46), channel_id=1, source_target_pairs={{0,32},{32,0},{64,96},{96,64},{128,160},{160,128},{192,224},{224,1... | collective-permute-start | bytes 5345288 | tf_op jit(solution)/shard_map/ppermute | solution.py:375
  9.3 3.5 %second.1 = (f32[1160,384]{1,0:T(8,128)S(1)}, bf16[1536,384]{1,0:T(8,128)(2,1)S(1)}, bf16[1536,384]{1,0:T(8,128)(2,1)S(1)}, f32[8,384]{1,0:T(8,128)S(1)}) custom-call(s32[1]{0:T(128)} %bitcast.refs_0_, f32[2,2,384]{2,1,0:T(2,128)S(1)} %get-tuple-element.47.refs_1_, bf16[2,2,384,384]{3,2,1,0:T(8,128)(2,1)S(1)} %get-tuple-element.48.refs_2_, ...), custom_call_target="tpu_custom_call" | custom-call | flops 1472200704 | tf_op jit(solution)/shard_map/second/pallas_call | solution.py:82
  16.1 1.4 %up_join.1 = (f32[384,384]{1,0:T(8,128)S(1)}, bf16[768,384]{1,0:T(8,128)(2,1)S(1)}, bf16[768,384]{1,0:T(8,128)(2,1)S(1)}, bf16[768,384]{1,0:T(8,128)(2,1)S(1)}, ...) custom-call(s32[1]{0:T(128)} %bitcast.refs_0_, ...), custom_call_target="tpu_custom_call" | custom-call | flops 339738624 | tf_op jit(solution)/shard_map/up_join/pallas_call | solution.py:82
  17.5 2.0 %collective-permute-start.8 = (f32[384,384]{1,0:T(8,128)S(1)}, f32[384,384]{1,0:T(8,128)S(1)}, u32[]{:S(2)}, u32[]{:S(2)}) collective-permute-start(f32[384,384]{1,0:T(8,128)S(1)} %get-tuple-element.64), channel_id=1, source_target_pairs={{384,320},{416,352},{256,192},{288,224},{128,64},{160,96},{385,321... | collective-permute-start | bytes 1769480 | tf_op jit(solution)/shard_map/ppermute | solution.py:387
  20.5 1.3 %collective-permute-start.3 = (f32[8,384]{1,0:T(8,128)S(1)}, f32[8,384]{1,0:T(8,128)S(1)}, u32[]{:S(2)}, u32[]{:S(2)}) collective-permute-start(f32[8,384]{1,0:T(8,128)S(1)} %step.3), channel_id=1, source_target_pairs={{64,128},{96,160},{65,129},{97,161},{66,130},{98,162},{67,131},{99... | collective-permute-start | bytes 36872 | tf_op jit(solution)/shard_map/ppermute | solution.py:395
  21.8 8.2 %collective-permute-done.3.refs_3_.refs_5_.refs_9_.refs_11_ = f32[8,384]{1,0:T(8,128)S(1)} collective-permute-done((f32[8,384]{1,0:T(8,128)S(1)}, f32[8,384]{1,0:T(8,128)S(1)}, u32[]{:S(2)}, u32[]{:S(2)}) %collective-permute-start.3) | collective-permute-done | bytes 12320 | tf_op jit(solution)/shard_map/ppermute | solution.py:395
  30.2 1.3 %collective-permute-start.4 = (f32[8,384]{1,0:T(8,128)S(1)}, f32[8,384]{1,0:T(8,128)S(1)}, u32[]{:S(2)}, u32[]{:S(2)}) collective-permute-start(f32[8,384]{1,0:T(8,128)S(1)} %step.4), channel_id=1, source_target_pairs={{128,192},{160,224},{129,193},{161,225},{130,194},{162,226},{131,1... | collective-permute-start | bytes 36872 | tf_op jit(solution)/shard_map/ppermute | solution.py:395
  31.6 1.4 %collective-permute-done.4.refs_4_.refs_6_.refs_10_.refs_12_ = f32[8,384]{1,0:T(8,128)S(1)} collective-permute-done((f32[8,384]{1,0:T(8,128)S(1)}, f32[8,384]{1,0:T(8,128)S(1)}, u32[]{:S(2)}, u32[]{:S(2)}) %collective-permute-start.4) | collective-permute-done | bytes 12320 | tf_op jit(solution)/shard_map/ppermute | solution.py:395
  37.7 1.3 %collective-permute-start.10 = (f32[8,384]{1,0:T(8,128)S(1)}, f32[8,384]{1,0:T(8,128)S(1)}, u32[]{:S(2)}, u32[]{:S(2)}) collective-permute-start(f32[8,384]{1,0:T(8,128)S(1)} %turn.1.refs_1_), channel_id=1, source_target_pairs={{384,320},{416,352},{256,192},{288,224},{128,64},{160,96},{385,321... | collective-permute-start | bytes 36872 | tf_op jit(solution)/shard_map/ppermute | solution.py:425
  42.2 1.2 %spread.1 = (f32[8,384]{1,0:T(8,128)S(1)}, f32[8,384]{1,0:T(8,128)}, f32[8,384]{1,0:T(8,128)S(1)}) custom-call(s32[1]{0:T(128)} %bitcast.refs_0_, bf16[768,384]{1,0:T(8,128)(2,1)S(1)} %get-tuple-element.53.refs_0_.refs_1_, f32[8,384]{1,0:T(8,128)S(1)} %get-tuple-element.54.refs_2_.refs_1_, bf16[768,384]{1,0:T(8,128)(2,1)S(1)} %get-tuple-element.55.refs_3_.refs_2_, ...), custom_call_target="tpu_custom_call" | custom-call | flops 2264924 | tf_op jit(solution)/shard_map/spread/pallas_call | solution.py:82
  43.4 1.9 %collective-permute-start.13 = (f32[8,384]{1,0:T(8,128)}, f32[8,384]{1,0:T(8,128)}, u32[]{:S(2)}, u32[]{:S(2)}) collective-permute-start(f32[8,384]{1,0:T(8,128)} %get-tuple-element.77), channel_id=1, source_target_pairs={{0,32},{32,0},{64,96},{96,64},{128,160},{160,128},{192,224},{224,1... | collective-permute-start | bytes 36872 | tf_op jit(solution)/shard_map/ppermute | solution.py:433
  46.5 1.3 %collective-permute-start.12 = (f32[8,384]{1,0:T(8,128)}, f32[8,384]{1,0:T(8,128)}, u32[]{:S(2)}, u32[]{:S(2)}) collective-permute-start(f32[8,384]{1,0:T(8,128)} %get-tuple-element.72), channel_id=1, source_target_pairs={{192,64},{224,96},{193,65},{225,97},{194,66},{226,98},{195,67},{22... | collective-permute-start | bytes 36872 | tf_op jit(solution)/shard_map/ppermute | solution.py:423
  47.8 1.3 %copy-done.1 = bf16[1536,384]{1,0:T(8,128)(2,1)S(1)} copy-done((bf16[1536,384]{1,0:T(8,128)(2,1)S(1)}, bf16[1536,384]{1,0:T(8,128)(2,1)}, u32[]{:S(2)}) %copy-start.1) | copy-done | bytes 1179672
  49.1 1.3 %copy-done.3 = bf16[1536,384]{1,0:T(8,128)(2,1)S(1)} copy-done((bf16[1536,384]{1,0:T(8,128)(2,1)S(1)}, bf16[1536,384]{1,0:T(8,128)(2,1)}, u32[]{:S(2)}) %copy-start.3) | copy-done | bytes 1179672
  52.5 1.5 %local.1 = (f32[2,2,384]{2,1,0:T(2,128)S(1)}, f32[2,8,384]{2,1,0:T(8,128)S(1)}) custom-call(s32[1]{0:T(128)} %bitcast.refs_0_, s32[1]{0:T(128)} %bitcast.1.refs_1_, s32[2,4]{1,0:T(2,128)S(1)} %copy-done.22, bf16[1536,384]{1,0:T(8,128)(2,1)S(1)} %copy-done.1, bf16[1536,384]{1,0:T(8,128)(2,1)S(1)} %copy-done.3, f32[8,384]{1,0:T(8,128)S(1)} %copy-done.15, ...), custom_call_target="tpu_custom_call" | custom-call | flops 5662310 | tf_op jit(solution)/shard_map/local/pallas_call | solution.py:82
  54.0 1.4 %collective-permute-start.15 = (f32[8,384]{1,0:T(8,128)}, f32[8,384]{1,0:T(8,128)S(1)}, u32[]{:S(2)}, u32[]{:S(2)}) collective-permute-start(f32[8,384]{1,0:T(8,128)} %get-tuple-element.72), channel_id=1, source_target_pairs={{448,384},{480,416},{320,256},{352,288},{192,128},{224,160},{449,3... | collective-permute-start | bytes 36872 | tf_op jit(solution)/shard_map/ppermute | solution.py:428
  55.4 1.2 %back_step.5 = (f32[8,384]{1,0:T(8,128)S(1)}, f32[8,384]{1,0:T(8,128)S(1)}) custom-call(bf16[768,384]{1,0:T(8,128)(2,1)S(1)} %get-tuple-element.65.refs_0_, f32[8,384]{1,0:T(8,128)S(1)} %turn.1.refs_1_, bf16[768,384]{1,0:T(8,128)(2,1)S(1)} %get-tuple-element.70.refs_2_, f32[8,384]{1,0:T(8,128)S(1)} %copy-done.11, f32[8,384]{1,0:T(8,128)S(1)} %copy-done.13, ...), custom_call_target="tpu_custom_call" | custom-call | flops 2264924 | tf_op jit(solution)/shard_map/back_step/pallas_call | solution.py:82
  57.3 16.7 %collective-permute-done.15.refs_5_ = f32[8,384]{1,0:T(8,128)S(1)} collective-permute-done((f32[8,384]{1,0:T(8,128)}, f32[8,384]{1,0:T(8,128)S(1)}, u32[]{:S(2)}, u32[]{:S(2)}) %collective-permute-start.15) | collective-permute-done | bytes 12320 | tf_op jit(solution)/shard_map/ppermute | solution.py:428
  74.3 1.9 %collective-permute-start.16 = (f32[8,384]{1,0:T(8,128)S(1)}, f32[8,384]{1,0:T(8,128)S(1)}, u32[]{:S(2)}, u32[]{:S(2)}) collective-permute-start(f32[8,384]{1,0:T(8,128)S(1)} %get-tuple-element.83), channel_id=1, source_target_pairs={{0,32},{32,0},{64,96},{96,64},{128,160},{160,128},{192,224},{224,1... | collective-permute-start | bytes 36872 | tf_op jit(solution)/shard_map/ppermute | solution.py:450
  77.4 1.3 %last.1 = (f32[2,2,384]{2,1,0:T(2,128)}, f32[8,384]{1,0:T(8,128)S(1)}, f32[8,384]{1,0:T(8,128)S(1)}) custom-call(s32[1]{0:T(128)} %bitcast.refs_0_, f32[8,384]{1,0:T(8,128)S(1)} %collective-permute-done.16.refs_1_, f32[8,384]{1,0:T(8,128)S(1)} %get-tuple-element.84.refs_2_, f32[2,2,384]{2,1,0:T(2,128)S(1)} %get-tuple-element.82.refs_6_.refs_3_, ...), custom_call_target="tpu_custom_call" | custom-call | flops 5662310 | tf_op jit(solution)/shard_map/last/pallas_call | solution.py:82
  78.7 3.4 %collective-permute-start.17 = (f32[8,384]{1,0:T(8,128)S(1)}, f32[8,384]{1,0:T(8,128)S(1)}, u32[]{:S(2)}, u32[]{:S(2)}) collective-permute-start(f32[8,384]{1,0:T(8,128)S(1)} %get-tuple-element.89.refs_1_), channel_id=1, source_target_pairs={{0,1},{2,3},{4,5},{6,7},{8,9},{10,11},{12,13},{14,15},{16,17},{18,... | collective-permute-start | bytes 36872 | tf_op jit(solution)/shard_map/ppermute | solution.py:457
  82.1 15.5 %collective-permute-start.18 = (f32[8,384]{1,0:T(8,128)S(1)}, f32[8,384]{1,0:T(8,128)S(1)}, u32[]{:S(2)}, u32[]{:S(2)}) collective-permute-start(f32[8,384]{1,0:T(8,128)S(1)} %get-tuple-element.89.refs_1_), channel_id=1, source_target_pairs={{1,2},{3,4},{5,6},{7,8},{9,10},{11,12},{13,14},{15,16},{17,18},{19... | collective-permute-start | bytes 36872 | tf_op jit(solution)/shard_map/ppermute | solution.py:458
  97.6 3.0 %collective-permute-done.18.refs_3_ = f32[8,384]{1,0:T(8,128)S(1)} collective-permute-done((f32[8,384]{1,0:T(8,128)S(1)}, f32[8,384]{1,0:T(8,128)S(1)}, u32[]{:S(2)}, u32[]{:S(2)}) %collective-permute-start.18) | collective-permute-done | bytes 12320 | tf_op jit(solution)/shard_map/ppermute | solution.py:458
  (81 shorter events, 19.1 us)
Async XLA Ops:
  7.3 7.1 %collective-permute-start = (f32[1160,384]{1,0:T(8,128)}, f32[1160,384]{1,0:T(8,128)S(1)}, u32[]{:S(2)}, u32[]{:S(2)}) collective-permute-start(f32[1160,384]{1,0:T(8,128)} %get-tuple-element.46), channel_id=1, source_target_pairs={{0,32},{32,0},{64,96},{96,64},{128,160},{160,128},{192,224},{224,1... | collective-permute-start | bytes 5345288 | tf_op jit(solution)/shard_map/ppermute | solution.py:375
  15.4 18.7 %collective-permute-start.1 = (f32[392,384]{1,0:T(8,128)S(1)}, f32[392,384]{1,0:T(8,128)S(1)}, u32[]{:S(2)}, u32[]{:S(2)}) collective-permute-start(f32[392,384]{1,0:T(8,128)S(1)} %get-tuple-element.52), channel_id=1, source_target_pairs={{256,320},{288,352},{384,448},{416,480},{257,321},{289,353},{385,4... | collective-permute-start | bytes 1806344 | tf_op jit(solution)/shard_map/ppermute | solution.py:389
  17.5 16.7 %copy-start.4 = (bf16[768,384]{1,0:T(8,128)(2,1)}, bf16[768,384]{1,0:T(8,128)(2,1)S(1)}, u32[]{:S(2)}) copy-start(bf16[768,384]{1,0:T(8,128)(2,1)S(1)} %get-tuple-element.63.refs_2_) | copy-start | bytes 1769476
  17.5 19.0 %collective-permute-start.8 = (f32[384,384]{1,0:T(8,128)S(1)}, f32[384,384]{1,0:T(8,128)S(1)}, u32[]{:S(2)}, u32[]{:S(2)}) collective-permute-start(f32[384,384]{1,0:T(8,128)S(1)} %get-tuple-element.64), channel_id=1, source_target_pairs={{384,320},{416,352},{256,192},{288,224},{128,64},{160,96},{385,321... | collective-permute-start | bytes 1769480 | tf_op jit(solution)/shard_map/ppermute | solution.py:387
  19.6 0.7 collective-permute-start.2
  20.5 9.5 %collective-permute-start.3 = (f32[8,384]{1,0:T(8,128)S(1)}, f32[8,384]{1,0:T(8,128)S(1)}, u32[]{:S(2)}, u32[]{:S(2)}) collective-permute-start(f32[8,384]{1,0:T(8,128)S(1)} %step.3), channel_id=1, source_target_pairs={{64,128},{96,160},{65,129},{97,161},{66,130},{98,162},{67,131},{99... | collective-permute-start | bytes 36872 | tf_op jit(solution)/shard_map/ppermute | solution.py:395
  30.2 2.7 %collective-permute-start.4 = (f32[8,384]{1,0:T(8,128)S(1)}, f32[8,384]{1,0:T(8,128)S(1)}, u32[]{:S(2)}, u32[]{:S(2)}) collective-permute-start(f32[8,384]{1,0:T(8,128)S(1)} %step.4), channel_id=1, source_target_pairs={{128,192},{160,224},{129,193},{161,225},{130,194},{162,226},{131,1... | collective-permute-start | bytes 36872 | tf_op jit(solution)/shard_map/ppermute | solution.py:395
  33.2 1.0 %collective-permute-start.5 = (f32[8,384]{1,0:T(8,128)S(1)}, f32[8,384]{1,0:T(8,128)S(1)}, u32[]{:S(2)}, u32[]{:S(2)}) collective-permute-start(f32[8,384]{1,0:T(8,128)S(1)} %step.5), channel_id=1, source_target_pairs={{192,320},{224,352},{193,321},{225,353},{194,322},{226,354},{195,3... | collective-permute-start | bytes 36872 | tf_op jit(solution)/shard_map/ppermute | solution.py:400
  35.2 1.5 %collective-permute-start.6 = (f32[8,384]{1,0:T(8,128)S(1)}, f32[8,384]{1,0:T(8,128)S(1)}, u32[]{:S(2)}, u32[]{:S(2)}) collective-permute-start(f32[8,384]{1,0:T(8,128)S(1)} %get-tuple-element.61), channel_id=1, source_target_pairs={{320,448},{352,480},{321,449},{353,481},{322,450},{354,482},{323,4... | collective-permute-start | bytes 36872 | tf_op jit(solution)/shard_map/ppermute | solution.py:400
  35.9 0.8 collective-permute-start.7
  37.7 2.7 %collective-permute-start.10 = (f32[8,384]{1,0:T(8,128)S(1)}, f32[8,384]{1,0:T(8,128)S(1)}, u32[]{:S(2)}, u32[]{:S(2)}) collective-permute-start(f32[8,384]{1,0:T(8,128)S(1)} %turn.1.refs_1_), channel_id=1, source_target_pairs={{384,320},{416,352},{256,192},{288,224},{128,64},{160,96},{385,321... | collective-permute-start | bytes 36872 | tf_op jit(solution)/shard_map/ppermute | solution.py:425
  39.1 1.4 %collective-permute-start.9 = (f32[8,384]{1,0:T(8,128)S(1)}, f32[8,384]{1,0:T(8,128)S(1)}, u32[]{:S(2)}, u32[]{:S(2)}) collective-permute-start(f32[8,384]{1,0:T(8,128)S(1)} %turn.1.refs_1_), channel_id=1, source_target_pairs={{448,320},{480,352},{449,321},{481,353},{450,322},{482,354},{451,3... | collective-permute-start | bytes 36872 | tf_op jit(solution)/shard_map/ppermute | solution.py:423
  41.4 3.9 %collective-permute-start.11 = (f32[8,384]{1,0:T(8,128)S(1)}, f32[8,384]{1,0:T(8,128)S(1)}, u32[]{:S(2)}, u32[]{:S(2)}) collective-permute-start(f32[8,384]{1,0:T(8,128)S(1)} %get-tuple-element.71), channel_id=1, source_target_pairs={{320,192},{352,224},{321,193},{353,225},{322,194},{354,226},{323,1... | collective-permute-start | bytes 36872 | tf_op jit(solution)/shard_map/ppermute | solution.py:423
  43.4 4.4 %collective-permute-start.13 = (f32[8,384]{1,0:T(8,128)}, f32[8,384]{1,0:T(8,128)}, u32[]{:S(2)}, u32[]{:S(2)}) collective-permute-start(f32[8,384]{1,0:T(8,128)} %get-tuple-element.77), channel_id=1, source_target_pairs={{0,32},{32,0},{64,96},{96,64},{128,160},{160,128},{192,224},{224,1... | collective-permute-start | bytes 36872 | tf_op jit(solution)/shard_map/ppermute | solution.py:433
  46.5 8.9 %collective-permute-start.12 = (f32[8,384]{1,0:T(8,128)}, f32[8,384]{1,0:T(8,128)}, u32[]{:S(2)}, u32[]{:S(2)}) collective-permute-start(f32[8,384]{1,0:T(8,128)} %get-tuple-element.72), channel_id=1, source_target_pairs={{192,64},{224,96},{193,65},{225,97},{194,66},{226,98},{195,67},{22... | collective-permute-start | bytes 36872 | tf_op jit(solution)/shard_map/ppermute | solution.py:423
  53.9 20.1 %copy-start.5 = (bf16[768,384]{1,0:T(8,128)(2,1)S(1)}, bf16[768,384]{1,0:T(8,128)(2,1)}, u32[]{:S(2)}) copy-start(bf16[768,384]{1,0:T(8,128)(2,1)} %copy-done.4) | copy-start | bytes 1769476
  53.9 20.1 %copy-start.21 = (f32[8,384]{1,0:T(8,128)S(1)}, f32[8,384]{1,0:T(8,128)}, u32[]{:S(2)}) copy-start(f32[8,384]{1,0:T(8,128)} %copy-done.20) | copy-start | bytes 36868
  54.0 23.4 %copy-start.6 = (bf16[384,384]{1,0:T(8,128)(2,1)S(1)}, bf16[384,384]{1,0:T(8,128)(2,1)}, u32[]{:S(2)}) copy-start(bf16[384,384]{1,0:T(8,128)(2,1)} %refs_6_.1) | copy-start | bytes 884740
  54.0 20.0 %collective-permute-start.15 = (f32[8,384]{1,0:T(8,128)}, f32[8,384]{1,0:T(8,128)S(1)}, u32[]{:S(2)}, u32[]{:S(2)}) collective-permute-start(f32[8,384]{1,0:T(8,128)} %get-tuple-element.72), channel_id=1, source_target_pairs={{448,384},{480,416},{320,256},{352,288},{192,128},{224,160},{449,3... | collective-permute-start | bytes 36872 | tf_op jit(solution)/shard_map/ppermute | solution.py:428
  56.6 17.4 %collective-permute-start.14 = (f32[8,384]{1,0:T(8,128)S(1)}, f32[8,384]{1,0:T(8,128)S(1)}, u32[]{:S(2)}, u32[]{:S(2)}) collective-permute-start(f32[8,384]{1,0:T(8,128)S(1)} %get-tuple-element.81), channel_id=1, source_target_pairs={{64,0},{96,32},{65,1},{97,33},{66,2},{98,34},{67,3},{99,35},{68,4}... | collective-permute-start | bytes 36872 | tf_op jit(solution)/shard_map/ppermute | solution.py:444
  74.3 3.1 %collective-permute-start.16 = (f32[8,384]{1,0:T(8,128)S(1)}, f32[8,384]{1,0:T(8,128)S(1)}, u32[]{:S(2)}, u32[]{:S(2)}) collective-permute-start(f32[8,384]{1,0:T(8,128)S(1)} %get-tuple-element.83), channel_id=1, source_target_pairs={{0,32},{32,0},{64,96},{96,64},{128,160},{160,128},{192,224},{224,1... | collective-permute-start | bytes 36872 | tf_op jit(solution)/shard_map/ppermute | solution.py:450
  77.4 23.3 %copy-start.7 = (bf16[384,384]{1,0:T(8,128)(2,1)S(1)}, bf16[384,384]{1,0:T(8,128)(2,1)}, u32[]{:S(2)}) copy-start(bf16[384,384]{1,0:T(8,128)(2,1)} %refs_5_.1) | copy-start | bytes 884740
  78.7 18.9 %collective-permute-start.17 = (f32[8,384]{1,0:T(8,128)S(1)}, f32[8,384]{1,0:T(8,128)S(1)}, u32[]{:S(2)}, u32[]{:S(2)}) collective-permute-start(f32[8,384]{1,0:T(8,128)S(1)} %get-tuple-element.89.refs_1_), channel_id=1, source_target_pairs={{0,1},{2,3},{4,5},{6,7},{8,9},{10,11},{12,13},{14,15},{16,17},{18,... | collective-permute-start | bytes 36872 | tf_op jit(solution)/shard_map/ppermute | solution.py:457
  82.1 18.5 %collective-permute-start.18 = (f32[8,384]{1,0:T(8,128)S(1)}, f32[8,384]{1,0:T(8,128)S(1)}, u32[]{:S(2)}, u32[]{:S(2)}) collective-permute-start(f32[8,384]{1,0:T(8,128)S(1)} %get-tuple-element.89.refs_1_), channel_id=1, source_target_pairs={{1,2},{3,4},{5,6},{7,8},{9,10},{11,12},{13,14},{15,16},{17,18},{19... | collective-permute-start | bytes 36872 | tf_op jit(solution)/shard_map/ppermute | solution.py:458
  (19 other events, 50.3 us)
